TPU v7x, 512 devices: a whole 4x8x8 slice. The times are simulated.
512 devices in a mesh: dp: 32 (over x, y), tensor: 16 (over z, core).
Axes of the slice: x: 4, y: 8, z: 8, core: 2. Of those that a mesh axis runs over, the one named last changes fastest.
Arguments:
- tokens: bfloat16 [4096, 8192], P('dp', 'tensor'), may hold values from -6 to 6
- base_weight: bfloat16 [8192, 8192], P('tensor', 'dp'), may hold values from -4 to 4
- adapter_down: bfloat16 [32, 16, 8192], P(None, None, 'tensor'), may hold values from -0.0625 to 0.0625
- adapter_up: bfloat16 [32, 16, 8192], P(None, None, 'dp'), may hold values from -1.5 to 1.5
- magnitude: float32 [32, 8192], P(None, 'tensor'), may hold values from 0.5 to 2
- tenant: int32 [16], replicated, may hold values from 0 to 31
- cotangent: bfloat16 [4096, 8192], P('dp', 'tensor'), may hold values from -0.29882812 to 0.29882812
Outputs:
- projected: bfloat16 [4096, 8192], P('dp', 'tensor')
- grad_down: float32 [32, 16, 8192], P(None, None, 'tensor')
- grad_up: float32 [32, 16, 8192], P(None, None, 'tensor')
- grad_magnitude: float32 [32, 8192], P(None, 'tensor')
All inputs are finite; a program needn't handle non-finite values.
Results may differ from a plain program's by a relative error of at most 0.001.
Values may be sent and summed in bfloat16 or wider, within the bound.
A program may use at most 64 MiB of HBM per device.

v0:
```python
import jax
import jax.numpy as jnp
from jax import lax
from jax.sharding import PartitionSpec as P

STRETCH = 256


def norm_terms(weight_rows, down_rows, up_rows):
    base_squares = jnp.sum(jnp.square(weight_rows.astype(jnp.float32)), axis=0)
    crossed = jnp.einsum("brk,kn->brn", down_rows, weight_rows, preferred_element_type=jnp.float32)
    gram_rows = jnp.einsum("brk,bsk->brs", down_rows, down_rows, preferred_element_type=jnp.float32)
    up_f32 = up_rows.astype(jnp.float32)
    crossed_sum = jnp.sum(up_f32 * crossed, axis=1)
    quadratic = jnp.sum(
        up_f32 * jnp.einsum("brs,bsn->brn", gram_rows, up_f32, precision=lax.Precision.HIGHEST),
        axis=1,
    )
    return base_squares[None, :] + 2.0 * crossed_sum + quadratic


def per_device(tokens, base_weight, adapter_down, adapter_up, magnitude, tenant, cotangent):
    tok_rows = tokens.shape[0]
    share = tokens.shape[1]
    tenants_all = adapter_down.shape[0]
    dp_count = lax.axis_size("dp")
    dp_index = lax.axis_index("dp")
    tensor_index = lax.axis_index("tensor")
    blocks_dev = max(tok_rows // STRETCH, 1)
    span_rows = min(tok_rows, STRETCH)
    starts = jnp.arange(dp_count, dtype=jnp.int32) * tok_rows // STRETCH
    index_all = starts[:, None] + jnp.arange(blocks_dev, dtype=jnp.int32)[None, :]
    stretch_ids = jnp.arange(tenant.shape[0], dtype=jnp.int32)
    tenants_grid = jnp.sum(
        jnp.where(index_all[:, :, None] == stretch_ids[None, None, :], tenant[None, None, :], 0),
        axis=-1,
    )
    tenants_own = lax.dynamic_index_in_dim(tenants_grid, dp_index, 0, keepdims=False)
    down_own = jnp.take(adapter_down, tenants_own, axis=0)
    up_selected = jnp.take(adapter_up, tenants_grid, axis=0)
    up_full = lax.all_to_all(up_selected, "dp", split_axis=0, concat_axis=3, tiled=True)[0]
    token_blocks = tokens.reshape(blocks_dev, span_rows, share)
    weight_full = lax.all_gather(base_weight, "dp", axis=1, tiled=True)
    rank_part = jnp.einsum(
        "cik,crk->cir", token_blocks, down_own, preferred_element_type=jnp.float32
    )
    square_part = norm_terms(weight_full, down_own, up_full)
    partial_value = jnp.dot(tokens, weight_full, preferred_element_type=jnp.float32)
    summed_base = lax.psum_scatter(partial_value, "tensor", scatter_dimension=1, tiled=True)
    out_cols = summed_base.shape[1]
    rank_acts, squares = lax.psum((rank_part, square_part), "tensor")
    column_norm = jnp.sqrt(
        lax.dynamic_slice_in_dim(squares, tensor_index * out_cols, out_cols, 1) + 1e-06
    )
    up_own = lax.dynamic_slice_in_dim(up_full, tensor_index * out_cols, out_cols, 2).astype(
        jnp.float32
    )
    low_rank = jnp.einsum("cir,crn->cin", rank_acts, up_own, precision=lax.Precision.HIGHEST)
    summed_blocks = summed_base.reshape(blocks_dev, span_rows, out_cols) + low_rank
    scaling = jnp.take(magnitude, tenants_own, axis=0) / column_norm
    projected = (
        (summed_blocks * scaling[:, None, :]).reshape(tok_rows, out_cols).astype(jnp.bfloat16)
    )
    cotan = cotangent.reshape(blocks_dev, span_rows, out_cols).astype(jnp.float32)
    scaled = cotan * scaling[:, None, :]
    up_terms = jnp.einsum("cir,cin->crn", rank_acts, scaled, precision=lax.Precision.HIGHEST)
    back_part = jnp.einsum("cin,crn->cir", scaled, up_own, precision=lax.Precision.HIGHEST)
    rank_back = lax.psum(back_part, "tensor")
    down_terms = jnp.einsum(
        "cir,cik->crk", rank_back, token_blocks.astype(jnp.float32), precision=lax.Precision.HIGHEST
    )
    mag_terms = jnp.sum(cotan * summed_blocks / column_norm[:, None, :], axis=1)
    tenant_range = jnp.arange(tenants_all, dtype=jnp.int32)
    onehot = (tenants_own[:, None] == tenant_range[None, :]).astype(jnp.float32)
    dense_down = jnp.einsum("ct,crk->trk", onehot, down_terms, precision=lax.Precision.HIGHEST)
    dense_up = jnp.einsum("ct,crn->trn", onehot, up_terms, precision=lax.Precision.HIGHEST)
    dense_mag = jnp.einsum("ct,cn->tn", onehot, mag_terms, precision=lax.Precision.HIGHEST)
    grad_down, grad_up, grad_magnitude = lax.psum((dense_down, dense_up, dense_mag), "dp")
    return (projected, grad_down, grad_up, grad_magnitude)


def solution(mesh):
    in_specs = (
        P("dp", "tensor"),
        P("tensor", "dp"),
        P(None, None, "tensor"),
        P(None, None, "dp"),
        P(None, "tensor"),
        P(),
        P("dp", "tensor"),
    )
    out_specs = (
        P("dp", "tensor"),
        P(None, None, "tensor"),
        P(None, None, "tensor"),
        P(None, "tensor"),
    )
    return jax.shard_map(
        per_device, mesh=mesh, in_specs=in_specs, out_specs=out_specs, check_vma=False
    )
```

profile of v0, /device:TPU:1, one launch (start us, length us, event | category | flops | bytes accessed | tf_op | source)
XLA Modules:
  0.0 429.1 jit_solution(11879257283542117184)
XLA Ops:
  7.2 0.7 all-gather.2.cloned.1.call-update
  8.0 115.0 %all-gather.2.cloned.1.call-done = bf16[512,8192]{1,0:T(8,128)(2,1)} async-done(((bf16[512,256]{1,0:T(8,128)(2,1)}), bf16[512,8192]{1,0:T(8,128)(2,1)}) %all-gather.2.cloned.1.call-update) | async-done | bytes 8388624 | tf_op jit(solution)/shard_map/all_gather | solution.py:43
  123.0 6.7 %fusion.26 = f32[128,8192]{1,0:T(8,128)} fusion(bf16[128,512]{1,0:T(8,128)(2,1)} %param.7, bf16[512,8192]{1,0:T(8,128)(2,1)} %all-gather.2.cloned.1.call-done), kind=kOutput, calls=%fused_computation.54 | convolution fusion | flops 1073741824 | bytes 12713984 | tf_op jit(solution)/shard_map/dot_general | solution.py:48
  129.8 0.6 gather_fusion
  130.4 0.8 bitcast_select_fusion
  131.2 4.9 %all-to-all-start = ((bf16[32,1,16,256]{3,2,1,0:T(8,128)(2,1)}), bf16[32,1,16,256]{3,2,1,0:T(8,128)(2,1)S(1)}, u32[]{:S(2)}, u32[]{:S(2)}) async-start(bf16[32,1,16,256]{3,2,1,0:T(8,128)(2,1)} %bitcast_select_fusion), calls=%async_computation.1 | async-start | bytes 524288 | tf_op jit(solution)/shard_map/all_to_all | solution.py:41
  136.2 0.6 squeeze.9
  138.8 0.7 compare_convert_fusion
  139.4 0.9 fusion.10
  140.4 0.9 convolution_bitcast_fusion
  141.2 4.6 %all-to-all-done = bf16[32,1,16,256]{3,2,1,0:T(8,128)(2,1)S(1)} async-done(((bf16[32,1,16,256]{3,2,1,0:T(8,128)(2,1)}), bf16[32,1,16,256]{3,2,1,0:T(8,128)(2,1)S(1)}, u32[]{:S(2)}, u32[]{:S(2)}) %all-to-all-start) | async-done | bytes 262176 | tf_op jit(solution)/shard_map/all_to_all | solution.py:41
  146.1 0.4 fusion
  146.5 4.7 %fusion.1 = f32[8192]{0:T(1024)S(1)} fusion(bf16[512,8192]{1,0:T(8,128)(2,1)} %all-gather.2.cloned.1.call-done, bf16[16,8192]{1,0:T(8,128)(2,1)S(1)} %bitcast.51, bf16[32,16,512]{2,1,0:T(8,128)(2,1)} %param.9, s32[]{:T(128)} %bitcast.1, pred[]{:T(512)} %bitcast), kind=kOutput, calls=%fused_computation.5 | convolution fusion | flops 134610944 | bytes 8700928 | tf_op jit(solution)/shard_map/brk,kn->brn/dot_general | solution.py:11
  151.3 5.4 %multiply_reduce_fusion = f32[8192]{0:T(1024)S(1)} fusion(bf16[512,8192]{1,0:T(8,128)(2,1)} %all-gather.2.cloned.1.call-done), kind=kLoop, calls=%fused_computation.1 | loop fusion | flops 12574720 | bytes 8421376 | tf_op jit(solution)/shard_map/reduce_sum | solution.py:10
  156.7 49.0 %psum.43 = f32[1,8192]{1,0:T(1,128)S(1)} all-reduce(f32[1,8192]{1,0:T(1,128)S(1)} %bitcast.52), channel_id=1, replica_groups=mesh['dp'=32,'tensor'=16] {'tensor'}, use_global_device_ids=true, to_apply=%region_6.7 | all-reduce | flops 8192 | bytes 65536 | tf_op jit(solution)/shard_map/psum | solution.py:51
  205.7 0.7 fusion.16
  206.7 45.8 %all-reduce.1 = (f32[128,16]{0,1:T(8,128)S(1)}, f32[128,16]{0,1:T(8,128)S(1)}) all-reduce(f32[128,16]{0,1:T(8,128)S(1)} %convolution_bitcast_fusion, f32[128,16]{0,1:T(8,128)S(1)} %fusion.3), channel_id=1, replica_groups=mesh['dp'=32,'tensor'=16] {'tensor'}, use_global_device_ids=true, to_apply=%region_2.3 | all-reduce | flops 4096 | bytes 32768 | tf_op jit(solution)/shard_map/psum | solution.py:51
  252.9 1.5 broadcast_multiply_fusion
  254.4 1.9 fusion.5
  256.3 0.7 broadcast_multiply_fusion.2
  257.1 159.4 %all-reduce.4.cloned.1.call-done = (f32[32,16,512]{2,1,0:T(8,128)}, f32[32,16,512]{2,1,0:T(8,128)}, f32[32,512]{1,0:T(8,128)}) async-done(((f32[32,16,512]{2,1,0:T(8,128)}, f32[32,16,512]{2,1,0:T(8,128)}, f32[32,512]{1,0:T(8,128)}), (f32[32,16,512]{2,1,0:T(8,128)}, f32[32,16,512]{2,1,0:T(8,128)}, f32[32,512]{1,0:T(8,128)})) %all-reduce.4.cloned.1.call-update) | async-done | bytes 2162704 | tf_op jit(solution)/shard_map/psum | solution.py:78
  416.5 2.3 copy.23
  418.8 2.3 copy.24
  421.1 1.5 copy.25
  (26 shorter events, 1.2 us)
Async XLA Ops:
  7.2 122.7 %copy-start = (bf16[32,16,256]{2,1,0:T(8,128)(2,1)S(1)}, bf16[32,16,256]{2,1,0:T(8,128)(2,1)}, u32[]{:S(2)}) copy-start(bf16[32,16,256]{2,1,0:T(8,128)(2,1)} %param.10) | copy-start | bytes 786436
  7.2 115.8 %all-gather.2.cloned.1.call-start = ((), (), s32[]{:S(2)}) async-start(), calls=%async_computation.2 | async-start | bytes 8650752 | tf_op jit(solution)/shard_map/all_gather | solution.py:43
  7.9 121.8 %copy-start.3 = (s32[16]{0:T(128)S(1)}, s32[16]{0:T(128)}, u32[]{:S(2)}) copy-start(s32[16]{0:T(128)} %param.12) | copy-start | bytes 196
  7.9 132.4 %copy-start.1 = (bf16[128,512]{1,0:T(8,128)(2,1)S(1)}, bf16[128,512]{1,0:T(8,128)(2,1)}, u32[]{:S(2)}) copy-start(bf16[128,512]{1,0:T(8,128)(2,1)} %param.7) | copy-start | bytes 393220
  7.9 246.5 %reduce-scatter.2.cloned.1.call-start = ((), (), s32[]{:S(2)}) async-start(), calls=%async_computation.3 | async-start | bytes 4456448 | tf_op jit(solution)/shard_map/reduce_scatter | solution.py:49
  131.2 14.6 %all-to-all-start = ((bf16[32,1,16,256]{3,2,1,0:T(8,128)(2,1)}), bf16[32,1,16,256]{3,2,1,0:T(8,128)(2,1)S(1)}, u32[]{:S(2)}, u32[]{:S(2)}) async-start(bf16[32,1,16,256]{3,2,1,0:T(8,128)(2,1)} %bitcast_select_fusion), calls=%async_computation.1 | async-start | bytes 524288 | tf_op jit(solution)/shard_map/all_to_all | solution.py:41
  136.2 280.3 %all-reduce.4.cloned.1.call-start = ((), (), s32[]{:S(2)}) async-start(), calls=%async_computation.4 | async-start | bytes 4325376 | tf_op jit(solution)/shard_map/psum | solution.py:78
  146.5 60.0 %copy-start.2 = (bf16[128,512]{1,0:T(8,128)(2,1)S(1)}, bf16[128,512]{1,0:T(8,128)(2,1)}, u32[]{:S(2)}) copy-start(bf16[128,512]{1,0:T(8,128)(2,1)} %param.13) | copy-start | bytes 393220
Sparse Core Ops, SparseCore 0:
  11.1 111.8 all-gather.1
  129.8 63.9 reduce-scatter.1
  257.2 159.2 all-reduce.3
where the time goes:
time: 432 us; the launch traced here: 429 us
  waiting for transfers between devices  280 us (65%)
  blocking collectives  94.8 us (22%)
  matrix products  16.2 us (4%)
  between operations  15.9 us (4%)
  other arithmetic  9.96 us (2%)
  local copies, waits for them, and re-layouts  7.48 us (2%)
  starting transfers between devices  5.06 us (1%)
    psum x1, waiting for transfers between devices, per_device(): lax.psum((dense_down, dense_up, dense_mag), 'dp')  159 us
    all_gather x1, waiting for transfers between devices, per_device(): weight_full = lax.all_gather(base_weight, 'dp', axis=1, tiled=True)  115 us
    psum x2, blocking collectives, per_device(): rank_acts, squares = lax.psum((rank_part, square_part), 'tensor')  94.8 us
  transfers between devices with their start and end apart: 4, of which 3 were waited for; matrix products, arithmetic and copies ran while one was open for 4% of the time, Pallas kernels for 0%

commit v1 on v0

v1 whole, which is shorter than its diff:
```python
import functools

import jax
import jax.numpy as jnp
from jax import lax
from jax.experimental import pallas as pl
from jax.experimental.pallas import tpu as pltpu
from jax.sharding import PartitionSpec as P

X_CHIPS = 4
RANK = 16
F32 = jnp.float32
BF16 = jnp.bfloat16


def send_to(src, dst, send_sem, recv_sem, device):
    return pltpu.make_async_remote_copy(
        src_ref=src,
        dst_ref=dst,
        send_sem=send_sem,
        recv_sem=recv_sem,
        device_id=device,
        device_id_type=pl.DeviceIdType.MESH,
    )


def split3(value):
    high = value.astype(BF16)
    rest = value - high.astype(F32)
    middle = rest.astype(BF16)
    low = (rest - middle.astype(F32)).astype(BF16)
    return high, middle, low


def dot_nn(a, b):
    return jnp.dot(a, b, preferred_element_type=F32)


def dot_nt(a, b):
    return lax.dot_general(a, b, (((1,), (1,)), ((), ())), preferred_element_type=F32)


def dot_tn(a, b):
    return lax.dot_general(a, b, (((0,), (0,)), ((), ())), preferred_element_type=F32)


def halves_of(flow, step, count):
    if step < count // 2 - 1:
        return (0, 1)
    return (flow,)


def exchange_kernel(
    nx, ny, nt,
    tenant, tok, w, down, up, mag, cot,
    proj_out, g_out, m_out,
    tok_g, w_g, up_sel, up_g, down_sel, cot_l, mag_s, mag_l,
    ex_s, ex_l, rank_p, parts, sib, ring,
    scaled_s, f_s, f_l, h_s, h_l, rank_s, u_s, g, proj_s, proj_l, m_s, m_g,
    tok_ss, tok_rs, w_ss, w_rs, up_ss, up_rs, cot_ss, cot_rs, mag_ss, mag_rs,
    ex_ss, ex_rs, sib_ss, sib_rs, ring_ss, ring_rs, f_ss, f_rs, h_ss, h_rs,
    u_ss, u_rs, gy_ss, gy_rs, gx_ss, gx_rs, pr_ss, pr_rs, m_ss, m_rs,
    my_ss, my_rs, mx_ss, mx_rs,
):
    s_per = ny // 2
    nz = nt // 2
    rpy = RANK // ny
    tb, kb = tok.shape
    cb = w.shape[1]
    dp = lax.axis_index("dp")
    t = lax.axis_index("tensor")
    x, y = lax.div(dp, ny), lax.rem(dp, ny)
    z, core = lax.div(t, 2), lax.rem(t, 2)
    xq, cl = lax.div(t, s_per), lax.rem(t, s_per)
    y_half, y_par = lax.div(y, 2), lax.rem(y, 2)
    at_home = y_half == cl

    def dev(x2, y2, t2):
        return (x2 * ny + y2, t2)

    def wrap(value, count):
        return lax.rem(value + 2 * count, count)

    def on_y(i):
        return dev(x, wrap(y + i, ny), t)

    def on_x(i):
        return dev(wrap(x + i, nx), y, t)

    def on_t(i):
        return dev(x, y, wrap(t + i, nt))

    def on_z(i):
        return dev(x, y, 2 * wrap(z + i, nz) + core)

    sibling = dev(x, y, 2 * z + 1 - core)
    swap = [dev(x, 2 * cl + p, s_per * xq + y_half) for p in (0, 1)]
    swap_own = dev(x, 2 * cl + y_par, s_per * xq + y_half)

    barrier = pltpu.get_barrier_semaphore()

    def greet(device):
        pl.semaphore_signal(barrier, inc=1, device_id=device, device_id_type=pl.DeviceIdType.MESH)

    @pl.loop(1, ny)
    def _(i):
        greet(on_y(i))

    @pl.loop(1, nx)
    def _(i):
        greet(on_x(i))

    @pl.loop(1, nt)
    def _(i):
        greet(on_t(i))

    for p in (0, 1):
        @pl.when(jnp.logical_not(jnp.logical_and(at_home, y_par == p)))
        def _():
            greet(swap[p])

    tok_g[y] = tok[...].reshape(2, tb // 2, kb)
    w_g[x] = w[...].reshape(2, kb // 2, cb)
    for c in range(nx * s_per):
        up_sel[c // s_per, c % s_per] = up[tenant[c]]
    up_g[x] = up_sel[x]
    for c in range(s_per):
        down_sel[pl.ds(c * RANK, RANK), :] = down[tenant[x * s_per + c]]
    row_ids = lax.broadcasted_iota(jnp.int32, mag.shape, 0)
    mag_row = jnp.sum(jnp.where(row_ids == tenant[x * s_per + y_half], mag[...], 0.0), axis=0, keepdims=True)
    for p in (0, 1):
        mag_s[p] = jnp.broadcast_to(mag_row[:, p * cb:(p + 1) * cb], (8, cb))
    ex_s[...] = jnp.zeros_like(ex_s)
    f_s[...] = jnp.zeros_like(f_s)
    m_s[...] = jnp.zeros_like(m_s)

    others = (ny - 1) + (nx - 1) + (nt - 1)

    @pl.when(at_home)
    def _():
        pl.semaphore_wait(barrier, others + 1)

    @pl.when(jnp.logical_not(at_home))
    def _():
        pl.semaphore_wait(barrier, others + 2)

    def tok_copy(flow, step, h):
        sign = 1 if flow == 0 else -1
        block = wrap(y - sign * step, ny)
        slot = tok_g.at[block, h]
        return send_to(slot, slot, tok_ss.at[flow, step, h], tok_rs.at[flow, step, h], on_y(sign))

    def tok_arrival(flow, step, h):
        sign = 1 if flow == 0 else -1
        slot = tok_g.at[wrap(y - sign * (step + 1), ny), h]
        return send_to(slot, slot, tok_ss.at[flow, step, h], tok_rs.at[flow, step, h], on_y(sign))

    def w_copy(flow, step, h):
        sign = 1 if flow == 0 else -1
        slot = w_g.at[wrap(x - sign * step, nx), h]
        return send_to(slot, slot, w_ss.at[flow, step, h], w_rs.at[flow, step, h], on_x(sign))

    def w_arrival(flow, step, h):
        sign = 1 if flow == 0 else -1
        slot = w_g.at[wrap(x - sign * (step + 1), nx), h]
        return send_to(slot, slot, w_ss.at[flow, step, h], w_rs.at[flow, step, h], on_x(sign))

    for h in (0, 1):
        for flow in (0, 1):
            if h in halves_of(flow, 0, ny):
                tok_copy(flow, 0, h).start()
            if h in halves_of(flow, 0, nx):
                w_copy(flow, 0, h).start()

    def up_copy(i):
        return send_to(up_sel.at[wrap(x + i, nx)], up_g.at[x], up_ss.at[i], up_rs.at[i], on_x(i))

    def up_arrival(i):
        slot = up_g.at[wrap(x - i, nx)]
        return send_to(slot, slot, up_ss.at[i], up_rs.at[i], on_x(i))

    for i in range(1, nx):
        up_copy(i).start()

    def cot_copy(p):
        return send_to(cot.at[:, pl.ds(p * cb, cb)], cot_l.at[y_par], cot_ss.at[p], cot_rs.at[y_par], swap[p])

    def cot_arrival(p):
        return send_to(cot_l.at[p], cot_l.at[p], cot_ss.at[p], cot_rs.at[p], swap[p])

    def mag_copy(p):
        return send_to(mag_s.at[p], mag_l.at[y_par], mag_ss.at[p], mag_rs.at[y_par], swap[p])

    def mag_arrival(p):
        return send_to(mag_l.at[p], mag_l.at[p], mag_ss.at[p], mag_rs.at[p], swap[p])

    stays = [jnp.logical_and(at_home, y_par == p) for p in (0, 1)]
    for p in (0, 1):
        @pl.when(jnp.logical_not(stays[p]))
        def _():
            cot_copy(p).start()
            mag_copy(p).start()

        @pl.when(stays[p])
        def _():
            cot_l[p] = cot[:, p * cb:(p + 1) * cb]
            mag_l[p] = mag_s[p]

    for step in range(ny // 2):
        for h in (0, 1):
            for flow in (0, 1):
                if h in halves_of(flow, step, ny):
                    tok_arrival(flow, step, h).wait_recv()
                    if step + 1 < ny // 2 and h in halves_of(flow, step + 1, ny):
                        tok_copy(flow, step + 1, h).start()
                if step < nx // 2 and h in halves_of(flow, step, nx):
                    w_arrival(flow, step, h).wait_recv()
                    if step + 1 < nx // 2 and h in halves_of(flow, step + 1, nx):
                        w_copy(flow, step + 1, h).start()
    for i in range(1, nx):
        up_arrival(i).wait_recv()

    def stretch_tokens(c):
        return tok_g[pl.ds(2 * c, 2)].reshape(2 * tb, kb)

    for c in range(s_per):
        rank_p[c] = dot_nt(down_sel[pl.ds(c * RANK, RANK), :], stretch_tokens(c))
    grams = []
    for c in range(s_per):
        rows = down_sel[pl.ds(c * RANK, RANK), :]
        grams.append(jnp.concatenate(split3(dot_nt(rows, rows)), axis=0))

    @pl.loop(0, nx)
    def _(xb):
        block = w_g[xb].reshape(kb, cb)
        block_f32 = block.astype(F32)
        base = jnp.sum(block_f32 * block_f32, axis=0, keepdims=True)
        crossed = dot_nn(down_sel[...], block)
        for c in range(s_per):
            rows = up_g[xb, c]
            quad = dot_tn(grams[c], jnp.concatenate([rows, rows, rows], axis=0))
            mixed = rows.astype(F32) * (2.0 * crossed[c * RANK:(c + 1) * RANK] + quad)
            squares = base + jnp.sum(mixed, axis=0, keepdims=True)
            own = rank_p[c]
            picked = own[0:rpy]
            for y2 in range(1, ny):
                picked = jnp.where(y == y2, own[y2 * rpy:(y2 + 1) * rpy], picked)
            slot = xb * s_per + c
            ex_s[slot, 0:1, :] = squares[:, :cb // 2]
            ex_s[slot, 1:2, :] = squares[:, cb // 2:]
            ex_s[slot, 2:2 + rpy, :] = picked[:, :tb]
            ex_s[slot, 2 + rpy:2 + 2 * rpy, :] = picked[:, tb:]

    def ex_copy(i):
        return send_to(ex_s.at[wrap(t + i, nt)], ex_l.at[t], ex_ss.at[i], ex_rs.at[i], on_t(i))

    def ex_arrival(i):
        slot = ex_l.at[wrap(t - i, nt)]
        return send_to(slot, slot, ex_ss.at[i], ex_rs.at[i], on_t(i))

    @pl.loop(1, nt)
    def _(i):
        ex_copy(i).start()

    ex_l[t] = ex_s[t]

    half = nz // 2

    def place(i):
        return wrap(z + half + (1 - 2 * lax.rem(i, 2)) * lax.div(i + 1, 2), nz)

    def product(slot):
        xb, c = lax.div(slot, s_per), lax.rem(slot, s_per)
        result = dot_nn(stretch_tokens(c), w_g[xb].reshape(kb, cb))
        for p in (0, 1):
            for j in (0, 1):
                parts[slot, 2 * p + j] = result[p * tb:(p + 1) * tb, j * (cb // 2):(j + 1) * (cb // 2)]

    def sib_copy(i):
        zb = place(i)
        return send_to(parts.at[2 * zb + 1 - core], sib.at[zb], sib_ss.at[i], sib_rs.at[i], sibling)

    def sib_arrival(i):
        slot = sib.at[place(i)]
        return send_to(slot, slot, sib_ss.at[i], sib_rs.at[i], sibling)

    @pl.loop(0, nz)
    def _(i):
        product(2 * place(i) + 1 - core)
        sib_copy(i).start()
        product(2 * place(i) + core)

    def ring_copy(flow, step, q):
        sign = 1 if flow == 0 else -1
        zb = wrap(z + sign * (half - step), nz)
        return send_to(
            parts.at[2 * zb + core, q], ring.at[flow, step, q],
            ring_ss.at[flow, step, q], ring_rs.at[flow, step, q], on_z(sign),
        )

    def ring_has(flow, step, q):
        return step > 0 or q // 2 == flow

    def ring_step(step, q):
        for flow in (0, 1):
            sign = 1 if flow == 0 else -1
            if not ring_has(flow, step, q):
                continue
            zb = wrap(z + sign * (half - step), nz)
            value = parts[2 * zb + core, q] + sib[zb, q]
            if step > 0 and ring_has(flow, step - 1, q):
                ring_copy(flow, step - 1, q).wait_recv()
                value = value + ring[flow, step - 1, q]
            parts[2 * zb + core, q] = value
            ring_copy(flow, step, q).start()

    def after_extras():
        @pl.loop(1, nt)
        def _(i):
            ex_arrival(i).wait_recv()

        for p in (0, 1):
            @pl.when(jnp.logical_not(stays[p]))
            def _():
                cot_arrival(p).wait_recv()
                mag_arrival(p).wait_recv()

        total = jnp.sum(ex_l[...], axis=0)
        squares = jnp.concatenate([total[0:1], total[1:2]], axis=1)
        norm = jnp.sqrt(squares + 1e-06)
        scaling = mag_l[0][0:1] / norm
        scaled = cot_l[...].reshape(2 * tb, cb).astype(F32) * scaling
        scaled_s[...] = scaled
        rows = up_g[xq, cl]
        pieces = split3(scaled)
        back = dot_nt(rows, pieces[0]) + (dot_nt(rows, pieces[1]) + dot_nt(rows, pieces[2]))
        for y2 in range(ny):
            f_s[y2, 0:2 * rpy, :] = total[2:2 + 2 * rpy]
            f_s[y2, 8:8 + rpy, :] = back[y2 * rpy:(y2 + 1) * rpy, :tb]
            f_s[y2, 8 + rpy:8 + 2 * rpy, :] = back[y2 * rpy:(y2 + 1) * rpy, tb:]

        @pl.loop(1, ny)
        def _(i):
            f_copy(i).start()

        f_l[y] = f_s[y]
        return norm, scaling

    def f_copy(i):
        return send_to(f_s.at[wrap(y + i, ny)], f_l.at[y], f_ss.at[i], f_rs.at[i], on_y(i))

    def f_arrival(i):
        slot = f_l.at[wrap(y - i, ny)]
        return send_to(slot, slot, f_ss.at[i], f_rs.at[i], on_y(i))

    def h_copy(i):
        return send_to(h_s, h_l.at[t], h_ss.at[i], h_rs.at[i], on_t(i))

    def h_arrival(i):
        slot = h_l.at[wrap(t - i, nt)]
        return send_to(slot, slot, h_ss.at[i], h_rs.at[i], on_t(i))

    def u_copy(p):
        return send_to(u_s.at[p], g.at[x, 2 * cl + p, y_par], u_ss.at[p], u_rs.at[y_par], swap[p])

    def u_arrival(p):
        slot = g.at[x, y, p]
        return send_to(slot, slot, u_ss.at[p], u_rs.at[p], swap[p])

    def after_f():
        @pl.loop(1, ny)
        def _(i):
            f_arrival(i).wait_recv()

        h_s[...] = jnp.sum(f_l[:, 8:16, :], axis=0)

        @pl.loop(1, nt)
        def _(i):
            h_copy(i).start()

        h_l[t] = h_s[...]
        for y2 in range(ny):
            rank_s[y2 * rpy:(y2 + 1) * rpy, :tb] = f_l[y2, 0:rpy, :]
            rank_s[y2 * rpy:(y2 + 1) * rpy, tb:] = f_l[y2, rpy:2 * rpy, :]
        a1, a2, a3 = split3(rank_s[...])
        b1, b2, b3 = split3(scaled_s[...])
        low = dot_nn(a3, b1) + dot_nn(a2, b2) + dot_nn(a1, b3)
        terms = dot_nn(a1, b1) + (dot_nn(a2, b1) + dot_nn(a1, b2) + low)
        for p in (0, 1):
            u_s[p, 0:8, :] = terms[8 * p:8 * p + 8, :cb // 2]
            u_s[p, 8:16, :] = terms[8 * p:8 * p + 8, cb // 2:]

            @pl.when(jnp.logical_not(stays[p]))
            def _():
                u_copy(p).start()

            @pl.when(stays[p])
            def _():
                g[x, y, p] = u_s[p]

    def gy_copy(i):
        slot = g.at[x, y]
        return send_to(slot, slot, gy_ss.at[i], gy_rs.at[i], on_y(i))

    def gy_arrival(i):
        slot = g.at[x, wrap(y - i, ny)]
        return send_to(slot, slot, gy_ss.at[i], gy_rs.at[i], on_y(i))

    def after_h():
        @pl.loop(1, nt)
        def _(i):
            h_arrival(i).wait_recv()

        for c in range(s_per):
            tile = h_l[c]
            for xb in range(1, nx):
                tile = tile + h_l[xb * s_per + c]
            stacked = jnp.concatenate([v.astype(F32) for v in split3(tile)] + [jnp.zeros_like(tile)], axis=0)
            stacked = stacked.astype(BF16)
            both = []
            for p in (0, 1):
                full = dot_nn(stacked, tok_g[2 * c + p].reshape(tb, kb))
                both.append(full[0:8] + (full[8:16] + full[16:24]))
            terms = both[0][0:rpy] + both[1][rpy:2 * rpy]
            for q in range(kb // 128):
                g[x, y, 2 + q // 2, 8 * (q % 2) + c * rpy:8 * (q % 2) + (c + 1) * rpy, :] = terms[:, 128 * q:128 * (q + 1)]
        for p in (0, 1):
            @pl.when(jnp.logical_not(stays[p]))
            def _():
                u_arrival(p).wait_recv()

        @pl.loop(1, ny)
        def _(i):
            gy_copy(i).start()

    def gx_copy(flow, step, h):
        sign = 1 if flow == 0 else -1
        slot = g.at[wrap(x - sign * step, nx), pl.ds(h * s_per, s_per)]
        return send_to(slot, slot, gx_ss.at[flow, step, h], gx_rs.at[flow, step, h], on_x(sign))

    def gx_arrival(flow, step, h):
        sign = 1 if flow == 0 else -1
        slot = g.at[wrap(x - sign * (step + 1), nx), pl.ds(h * s_per, s_per)]
        return send_to(slot, slot, gx_ss.at[flow, step, h], gx_rs.at[flow, step, h], on_x(sign))

    def after_gy():
        @pl.loop(1, ny)
        def _(i):
            gy_arrival(i).wait_recv()

        for flow in (0, 1):
            for h in halves_of(flow, 0, nx):
                gx_copy(flow, 0, h).start()

    def after_gx(step):
        for h in (0, 1):
            for flow in (0, 1):
                if h in halves_of(flow, step, nx):
                    gx_arrival(flow, step, h).wait_recv()
                    if step + 1 < nx // 2 and h in halves_of(flow, step + 1, nx):
                        gx_copy(flow, step + 1, h).start()

    sib_arrival(0).wait_recv()
    for q in range(4):
        ring_step(0, q)
    norm, scaling = after_extras()
    for step in range(1, half):
        sib_arrival(2 * step - 1).wait_recv()
        sib_arrival(2 * step).wait_recv()
        for q in range(4):
            ring_step(step, q)
            if step == 1 and q == 1:
                after_f()
            if step == 2 and q == 0:
                after_h()
            if step == 2 and q == 3:
                after_gy()
    if half < 3:
        if half < 2:
            after_f()
        after_h()
        after_gy()
    sib_arrival(nz - 1).wait_recv()

    rank_stack = jnp.concatenate(split3(rank_s[...]), axis=0)
    rows = up_g[xq, cl]
    low_rank = dot_tn(rank_stack, jnp.concatenate([rows, rows, rows], axis=0))
    mag_sum = [None, None]
    for q in range(4):
        p, j = q // 2, q % 2
        value = parts[t, q] + sib[z, q]
        for flow in (0, 1):
            if ring_has(flow, half - 1, q):
                ring_copy(flow, half - 1, q).wait_recv()
                value = value + ring[flow, half - 1, q]
        lanes = slice(j * (cb // 2), (j + 1) * (cb // 2))
        value = value + low_rank[p * tb:(p + 1) * tb, lanes]
        proj_s[p, :, lanes] = (value * scaling[:, lanes]).astype(BF16)
        term = jnp.sum(cot_l[p, :, lanes].astype(F32) * value, axis=0, keepdims=True)
        mag_sum[j] = term if mag_sum[j] is None else mag_sum[j] + term

    def pr_copy(p):
        return send_to(proj_s.at[p], proj_l.at[y_par], pr_ss.at[p], pr_rs.at[y_par], swap[p])

    def pr_arrival(p):
        return send_to(proj_l.at[p], proj_l.at[p], pr_ss.at[p], pr_rs.at[p], swap[p])

    for j in (0, 1):
        m_s[j:j + 1, :] = mag_sum[j] / norm[:, j * (cb // 2):(j + 1) * (cb // 2)]

    def m_copy():
        return send_to(m_s, m_g.at[x, 2 * cl + y_par], m_ss, m_rs, swap_own)

    def m_arrival():
        slot = m_g.at[x, y]
        return send_to(slot, slot, m_ss, m_rs, swap_own)

    @pl.when(jnp.logical_not(at_home))
    def _():
        m_copy().start()

    @pl.when(at_home)
    def _():
        m_g[x, y] = m_s[...]

    for p in (0, 1):
        @pl.when(jnp.logical_not(stays[p]))
        def _():
            pr_copy(p).start()

        @pl.when(stays[p])
        def _():
            proj_l[p] = proj_s[p]

    for step in range(nx // 2):
        after_gx(step)

    def my_copy(i):
        slot = m_g.at[x, y]
        return send_to(slot, slot, my_ss.at[i], my_rs.at[i], on_y(i))

    def my_arrival(i):
        slot = m_g.at[x, wrap(y - i, ny)]
        return send_to(slot, slot, my_ss.at[i], my_rs.at[i], on_y(i))

    def mx_copy(i):
        slot = m_g.at[x]
        return send_to(slot, slot, mx_ss.at[i], mx_rs.at[i], on_x(i))

    def mx_arrival(i):
        slot = m_g.at[wrap(x - i, nx)]
        return send_to(slot, slot, mx_ss.at[i], mx_rs.at[i], on_x(i))

    @pl.when(jnp.logical_not(at_home))
    def _():
        m_arrival().wait_recv()

    @pl.loop(1, ny)
    def _(i):
        my_copy(i).start()

    g_out[...] = g[...]
    for p in (0, 1):
        @pl.when(jnp.logical_not(stays[p]))
        def _():
            pr_arrival(p).wait_recv()

        proj_out[:, p * cb:(p + 1) * cb] = proj_l[p]

    @pl.loop(1, ny)
    def _(i):
        my_arrival(i).wait_recv()

    @pl.loop(1, nx)
    def _(i):
        mx_copy(i).start()

    for flow in (0, 1):
        for step in range(ny // 2):
            for h in halves_of(flow, step, ny):
                tok_copy(flow, step, h).wait_send()
        for step in range(nx // 2):
            for h in halves_of(flow, step, nx):
                w_copy(flow, step, h).wait_send()
                gx_copy(flow, step, h).wait_send()
        for step in range(half):
            for q in range(4):
                if ring_has(flow, step, q):
                    ring_copy(flow, step, q).wait_send()

    @pl.loop(1, nt)
    def _(i):
        ex_copy(i).wait_send()
        h_copy(i).wait_send()

    @pl.loop(0, nz)
    def _(i):
        sib_copy(i).wait_send()

    @pl.loop(1, ny)
    def _(i):
        f_copy(i).wait_send()
        gy_copy(i).wait_send()
        my_copy(i).wait_send()

    for p in (0, 1):
        @pl.when(jnp.logical_not(stays[p]))
        def _():
            cot_copy(p).wait_send()
            mag_copy(p).wait_send()
            u_copy(p).wait_send()
            pr_copy(p).wait_send()

    @pl.when(jnp.logical_not(at_home))
    def _():
        m_copy().wait_send()

    for i in range(1, nx):
        up_copy(i).wait_send()

    @pl.loop(1, nx)
    def _(i):
        mx_arrival(i).wait_recv()
        mx_copy(i).wait_send()

    m_out[...] = m_g[...]


def scatter_kernel(nx, ny, tenant, proj, g, m, proj_out, down_out, up_out, mag_out):
    s_per = ny // 2
    rpy = RANK // ny
    proj_out[...] = proj[...]
    down_out[...] = jnp.zeros_like(down_out)
    up_out[...] = jnp.zeros_like(up_out)
    row_ids = lax.broadcasted_iota(jnp.int32, (mag_out.shape[0], 128), 0)
    mag_sums = [jnp.zeros(row_ids.shape, F32)] * (mag_out.shape[1] // 128)
    quarters = up_out.shape[2] // 128
    for xb in range(nx):
        for c in range(s_per):
            who = tenant[xb * s_per + c]
            for p in (0, 1):
                for q in range(quarters):
                    up_out[who, 8 * p:8 * p + 8, 128 * q:128 * (q + 1)] += g[
                        xb, 2 * c + p, q // 2, 8 * (q % 2):8 * (q % 2) + 8, :
                    ]
            for q in range(quarters):
                rows = [
                    g[xb, yb, 2 + q // 2, 8 * (q % 2) + c * rpy:8 * (q % 2) + (c + 1) * rpy, :]
                    for yb in range(ny)
                ]
                down_out[who, :, 128 * q:128 * (q + 1)] += jnp.concatenate(rows, axis=0)
                row = m[xb, 2 * c + q // 2, q % 2:q % 2 + 1, :]
                mag_sums[q] = mag_sums[q] + jnp.where(row_ids == who, row, 0.0)
    for q in range(quarters):
        mag_out[:, 128 * q:128 * (q + 1)] = mag_sums[q]


def per_device(nx, ny, nt, tokens, base_weight, adapter_down, adapter_up, magnitude, tenant, cotangent):
    tb, kb = tokens.shape
    cb = base_weight.shape[1]
    tenants = adapter_down.shape[0]
    s_per = ny // 2
    nz = nt // 2
    rpy = RANK // ny
    ex_rows = -(-(2 + 2 * rpy) // 8) * 8
    dma = pltpu.SemaphoreType.DMA
    vmem = pl.BlockSpec(memory_space=pltpu.VMEM)
    smem = pl.BlockSpec(memory_space=pltpu.SMEM)
    scratch = [
        pltpu.VMEM((ny, 2, tb // 2, kb), BF16),
        pltpu.VMEM((nx, 2, kb // 2, cb), BF16),
        pltpu.VMEM((nx, s_per, RANK, cb), BF16),
        pltpu.VMEM((nx, s_per, RANK, cb), BF16),
        pltpu.VMEM((s_per * RANK, kb), BF16),
        pltpu.VMEM((2, tb, cb), BF16),
        pltpu.VMEM((2, 8, cb), F32),
        pltpu.VMEM((2, 8, cb), F32),
        pltpu.VMEM((nt, ex_rows, 128), F32),
        pltpu.VMEM((nt, ex_rows, 128), F32),
        pltpu.VMEM((s_per, RANK, 2 * tb), F32),
        pltpu.VMEM((nt, 4, tb, cb // 2), F32),
        pltpu.VMEM((nz, 4, tb, cb // 2), F32),
        pltpu.VMEM((2, nz // 2, 4, tb, cb // 2), F32),
        pltpu.VMEM((2 * tb, cb), F32),
        pltpu.VMEM((ny, 16, 128), F32),
        pltpu.VMEM((ny, 16, 128), F32),
        pltpu.VMEM((8, 128), F32),
        pltpu.VMEM((nt, 8, 128), F32),
        pltpu.VMEM((RANK, 2 * tb), F32),
        pltpu.VMEM((2, 16, 128), F32),
        pltpu.VMEM((nx, ny, 4, 16, 128), F32),
        pltpu.VMEM((2, tb, cb), BF16),
        pltpu.VMEM((2, tb, cb), BF16),
        pltpu.VMEM((8, 128), F32),
        pltpu.VMEM((nx, ny, 8, 128), F32),
    ]
    sems = [
        (2, ny // 2, 2), (2, nx // 2, 2), (nx,), (2,), (2,),
        (nt,), (nz,), (2, nz // 2, 4), (ny,), (nt,),
        (2,), (ny,), (2, nx // 2, 2), (2,), None,
        (ny,), (nx,),
    ]
    for shape in sems:
        scratch += [dma if shape is None else dma(shape)] * 2
    proj, gathered, mags = pl.pallas_call(
        functools.partial(exchange_kernel, nx, ny, nt),
        out_shape=(
            jax.ShapeDtypeStruct((tb, 2 * cb), BF16),
            jax.ShapeDtypeStruct((nx, ny, 4, 16, 128), F32),
            jax.ShapeDtypeStruct((nx, ny, 8, 128), F32),
        ),
        in_specs=[smem] + [vmem] * 6,
        out_specs=(vmem, vmem, vmem),
        scratch_shapes=scratch,
        compiler_params=pltpu.CompilerParams(
            collective_id=0, has_side_effects=True, vmem_limit_bytes=32 * 1024 * 1024
        ),
        name="exchange",
    )(tenant, tokens, base_weight, adapter_down, adapter_up, magnitude, cotangent)
    return pl.pallas_call(
        functools.partial(scatter_kernel, nx, ny),
        out_shape=(
            jax.ShapeDtypeStruct((tb, 2 * cb), BF16),
            jax.ShapeDtypeStruct((tenants, RANK, kb), F32),
            jax.ShapeDtypeStruct((tenants, RANK, 2 * cb), F32),
            jax.ShapeDtypeStruct((tenants, 2 * cb), F32),
        ),
        in_specs=[smem, vmem, vmem, vmem],
        out_specs=(vmem, vmem, vmem, vmem),
        compiler_params=pltpu.CompilerParams(vmem_limit_bytes=16 * 1024 * 1024),
        name="scatter",
    )(tenant, proj, gathered, mags)


def solution(mesh, nx=X_CHIPS):
    ny = mesh.shape["dp"] // nx
    nt = mesh.shape["tensor"]
    in_specs = (
        P("dp", "tensor"),
        P("tensor", "dp"),
        P(None, None, "tensor"),
        P(None, None, "dp"),
        P(None, "tensor"),
        P(),
        P("dp", "tensor"),
    )
    out_specs = (
        P("dp", "tensor"),
        P(None, None, "tensor"),
        P(None, None, "tensor"),
        P(None, "tensor"),
    )
    return jax.shard_map(
        functools.partial(per_device, nx, ny, nt),
        mesh=mesh, in_specs=in_specs, out_specs=out_specs, check_vma=False,
    )
```

time: 432 us -> 97.6 us (0.23)
  waiting for transfers between devices: 280 us -> 0 us
  blocking collectives: 94.8 us -> 0 us
  Pallas kernels: 0 us -> 90 us
  matrix products: 16.2 us -> 0 us
  between operations: 15.9 us -> 0.66 us
  other arithmetic: 9.96 us -> 0 us
  starting transfers between devices: 5.06 us -> 0 us
    psum x1 -> x0, waiting for transfers between devices: 159 us -> none  [per_device(): lax.psum((dense_down, dense_up, dense_mag), 'dp')]
    all_gather x1 -> x0, waiting for transfers between devices: 115 us -> none  [per_device(): weight_full = lax.all_gather(base_weight, 'dp', axis=1, tiled=True)]
    psum x2 -> x0, blocking collectives: 94.8 us -> none  [per_device(): rank_acts, squares = lax.psum((rank_part, square_part), 'tensor')]
    pallas_call x0 -> x2, Pallas kernels: none -> 90 us  [the longest x1 87.8 us: per_device(): pl.pallas_call(functools.partial(exchange_kernel, nx, ny, nt), out_shape=...]
    dot_general x9 -> x0, matrix products: 16.2 us -> none  [the longest x1 6.7 us: per_device(): jnp.dot(tokens, weight_full, preferred_element_type=jnp.float32)]
    reduce_sum x2 -> x0, other arithmetic: 5.5 us -> none  [the longest x1 5.41 us: norm_terms(): base_squares = jnp.sum(jnp.square(weight_rows.astype(jnp.float32)), axis=0)]
    all_to_all x1 -> x0, starting transfers between devices: 4.94 us -> none  [per_device(): lax.all_to_all(up_selected, 'dp', split_axis=0, concat_axis=3, tiled=True)]
    all_to_all x1 -> x0, waiting for transfers between devices: 4.62 us -> none  [per_device(): lax.all_to_all(up_selected, 'dp', split_axis=0, concat_axis=3, tiled=True)]
  transfers between devices with their start and end apart: 4 -> 0, of which waited for: 3 -> 0; matrix products, arithmetic and copies ran while one was open for 4% -> 0% of each run, Pallas kernels for 0% -> 0%
where the time goes in v1:
time: 97.6 us; the launch traced here: 96.9 us
  Pallas kernels  90 us (92%)
  local copies, waits for them, and re-layouts  6.23 us (6%)
    pallas_call x1, Pallas kernels, per_device(): pl.pallas_call(functools.partial(exchange_kernel, nx, ny, nt), out_shape=...  87.8 us
    unnamed x14, local copies, waits for them, and re-layouts  6.23 us
    pallas_call x1, Pallas kernels, per_device(): pl.pallas_call(functools.partial(scatter_kernel, nx, ny), out_shape=(jax....  2.23 us

profile of v1, /device:TPU:1, one launch (start us, length us, event | category | flops | bytes accessed | tf_op | source)
XLA Modules:
  0.0 96.9 jit_solution(9944051385808657090)
XLA Ops:
  0.6 0.0 copy-start
  0.6 1.0 %copy-done = bf16[32,16,512]{2,1,0:T(8,128)(2,1)S(1)} copy-done((bf16[32,16,512]{2,1,0:T(8,128)(2,1)S(1)}, bf16[32,16,512]{2,1,0:T(8,128)(2,1)}, u32[]{:S(2)}) %copy-start) | copy-done | bytes 524312
  1.7 0.0 copy-start.1
  1.7 0.9 copy-done.1
  2.6 0.0 copy-start.2
  2.6 0.9 copy-done.2
  3.6 0.0 copy-start.3
  3.6 0.9 copy-done.3
  4.5 0.0 copy-start.4
  4.5 0.9 copy-done.4
  5.4 0.0 copy-start.5
  5.4 0.8 copy-done.5
  6.2 0.0 copy-start.6
  6.2 0.7 copy-done.6
  6.9 87.8 %exchange.1 = (bf16[128,512]{1,0:T(8,128)(2,1)S(1)}, f32[4,8,4,16,128]{4,3,2,1,0:T(8,128)S(1)}, f32[4,8,8,128]{3,2,1,0:T(8,128)S(1)}) custom-call(s32[16]{0:T(128)S(1)} %copy-done.6, bf16[128,512]{1,0:T(8,128)(2,1)S(1)} %copy-done.3, bf16[512,256]{1,0:T(8,128)(2,1)S(1)} %copy-done.1, bf16[32,16,512]{2,1,0:T(8,128)(2,1)S(1)} %copy-done, ...), custom_call_target="tpu_custom_call" | custom-call | tf_op jit(solution)/shard_map/exchange/pallas_call | solution.py:705
  94.7 2.2 %scatter.1 = (bf16[128,512]{1,0:T(8,128)(2,1)}, f32[32,16,512]{2,1,0:T(8,128)}, f32[32,16,512]{2,1,0:T(8,128)}, f32[32,512]{1,0:T(8,128)}) custom-call(s32[16]{0:T(128)S(1)} %copy-done.6, bf16[128,512]{1,0:T(8,128)(2,1)S(1)} %get-tuple-element.7.proj, f32[4,8,4,16,128]{4,3,2,1,0:T(8,128)S(1)} %get-tuple-element.8.g, f32[4,8,8,128]{3,2,1,0:T(8,128)S(1)} %get-tuple-element.9.m), custom_call_target="tpu_custom_call" | custom-call | tf_op jit(solution)/shard_map/scatter/pallas_call | solution.py:720
Async XLA Ops:
  0.6 1.0 %copy-start = (bf16[32,16,512]{2,1,0:T(8,128)(2,1)S(1)}, bf16[32,16,512]{2,1,0:T(8,128)(2,1)}, u32[]{:S(2)}) copy-start(bf16[32,16,512]{2,1,0:T(8,128)(2,1)} %down.1) | copy-start | bytes 1572868
  1.7 0.9 copy-start.1
  2.6 0.9 copy-start.2
  3.6 0.9 copy-start.3
  4.5 0.9 copy-start.4
  5.4 0.8 copy-start.5
  6.2 0.7 copy-start.6

commit v2 on v0

v2 whole, which is shorter than its diff:
```python
import functools

import jax
import jax.numpy as jnp
from jax import lax
from jax.experimental import pallas as pl
from jax.experimental.pallas import tpu as pltpu
from jax.sharding import PartitionSpec as P

X_CHIPS = 4
RANK = 16
F32 = jnp.float32
BF16 = jnp.bfloat16


def send_to(src, dst, send_sem, recv_sem, device):
    return pltpu.make_async_remote_copy(
        src_ref=src,
        dst_ref=dst,
        send_sem=send_sem,
        recv_sem=recv_sem,
        device_id=device,
        device_id_type=pl.DeviceIdType.MESH,
    )


def split3(value):
    high = value.astype(BF16)
    rest = value - high.astype(F32)
    middle = rest.astype(BF16)
    low = (rest - middle.astype(F32)).astype(BF16)
    return high, middle, low


def dot_nn(a, b):
    return jnp.dot(a, b, preferred_element_type=F32)


def dot_nt(a, b):
    return lax.dot_general(a, b, (((1,), (1,)), ((), ())), preferred_element_type=F32)


def dot_tn(a, b):
    return lax.dot_general(a, b, (((0,), (0,)), ((), ())), preferred_element_type=F32)


def halves(flow, step, count, pieces):
    if step < count // 2 - 1:
        return tuple(range(pieces))
    return tuple(range(pieces // 2)) if flow == 0 else tuple(range(pieces // 2, pieces))


def send_order(flow, step, count, pieces):
    chosen = halves(flow, step, count, pieces)
    if flow == 1 and len(chosen) == pieces:
        chosen = chosen[pieces // 2:] + chosen[:pieces // 2]
    return chosen


def exchange_kernel(
    nx, ny, nt,
    tenant, tok, w, down, up, mag, cot,
    proj_out, gu_out, gd_out, m_out,
    down_v, up_v, mag_v, cot_v, tok_g, w_g, up_sel, up_g, down_sel, cot_l, mag_s, mag_l,
    ex_s, ex_l, rk_s, rk_l, rank_p, parts, sib, ring,
    scaled_s, f_s, f_l, r_s, r_l, h_s, h_l, rank_s, u_s, gu, gd, low_s, proj_s, proj_l, m_s, m_g,
    in_s, tok_ss, tok_rs, w_ss, w_rs, up_ss, up_rs, cot_ss, cot_rs, mag_ss, mag_rs,
    ex_ss, ex_rs, rk_ss, rk_rs, sib_ss, sib_rs, ring_ss, ring_rs, f_ss, f_rs, r_ss, r_rs, h_ss, h_rs,
    u_ss, u_rs, ux_ss, ux_rs, dy_ss, dy_rs, dx_ss, dx_rs, pr_ss, pr_rs, m_ss, m_rs, out_s,
):
    s_per = ny // 2
    nz = nt // 2
    half = nz // 2
    rpy = RANK // ny
    tb, kb = tok.shape
    cb = w.shape[1]
    hb = cb // 2
    dp = lax.axis_index("dp")
    t = lax.axis_index("tensor")
    x, y = lax.div(dp, ny), lax.rem(dp, ny)
    z, core = lax.div(t, 2), lax.rem(t, 2)
    xq, cl = lax.div(t, s_per), lax.rem(t, s_per)
    y_half, y_par = lax.div(y, 2), lax.rem(y, 2)
    at_home = y_half == cl
    away = jnp.logical_not(at_home)
    t_out = s_per * xq + y_half

    def dev(x2, y2, t2):
        return (x2 * ny + y2, t2)

    def wrap(value, count):
        return lax.rem(value + 2 * count, count)

    def on_y(i):
        return dev(x, wrap(y + i, ny), t)

    def on_x(i):
        return dev(wrap(x + i, nx), y, t)

    def on_t(i):
        return dev(x, y, wrap(t + i, nt))

    def on_z(i):
        return dev(x, y, 2 * wrap(z + i, nz) + core)

    def on_swap(p):
        return dev(x, 2 * cl + p, t_out)

    sibling = dev(x, y, 2 * z + 1 - core)
    stays = [jnp.logical_and(at_home, y_par == p) for p in (0, 1)]

    fetches = [
        pltpu.make_async_copy(src, dst, in_s.at[n])
        for n, (src, dst) in enumerate((
            (w, w_g.at[x]), (up, up_v), (down, down_v), (mag, mag_v), (tok, tok_g.at[y]), (cot, cot_v),
        ))
    ]
    for fetch in fetches:
        fetch.start()
    barrier = pltpu.get_barrier_semaphore()

    def greet(device):
        pl.semaphore_signal(barrier, inc=1, device_id=device, device_id_type=pl.DeviceIdType.MESH)

    @pl.loop(1, ny)
    def _(i):
        greet(on_y(i))

    @pl.loop(1, nx)
    def _(i):
        greet(on_x(i))

    @pl.loop(1, nt)
    def _(i):
        greet(on_t(i))

    outs = nx * ny

    def source(i):
        xb, rest = lax.div(i, ny), lax.rem(i, ny)
        return dev(xb, 2 * cl + lax.rem(rest, 2), s_per * xq + lax.div(rest, 2))

    own_source = x * ny + 2 * cl + y_par

    def target(i):
        return (i, t_out)

    @pl.loop(0, outs)
    def _(i):
        @pl.when(jnp.logical_not(jnp.logical_and(at_home, i == own_source)))
        def _():
            greet(source(i))

    for fetch in fetches[1:4]:
        fetch.wait()
    for c in range(nx * s_per):
        up_sel[c // s_per, c % s_per] = up_v[tenant[c]]
    up_g[x] = up_sel[x]
    for c in range(s_per):
        down_sel[c] = down_v[tenant[x * s_per + c]]
    row_ids = lax.broadcasted_iota(jnp.int32, mag_v.shape, 0)
    mag_row = jnp.sum(jnp.where(row_ids == tenant[x * s_per + y_half], mag_v[...], 0.0), axis=0, keepdims=True)
    for p in (0, 1):
        mag_s[p] = jnp.broadcast_to(mag_row[:, p * cb:(p + 1) * cb], (8, cb))

    others = (ny - 1) + (nx - 1) + (nt - 1)

    @pl.when(at_home)
    def _():
        pl.semaphore_wait(barrier, others + outs - 1)

    @pl.when(away)
    def _():
        pl.semaphore_wait(barrier, others + outs)

    pieces = 4
    tp, wp = tb // pieces, kb // pieces

    def sign_of(flow):
        return 1 if flow == 0 else -1

    def tok_copy(flow, step, h):
        sign = sign_of(flow)
        slot = tok_g.at[wrap(y - sign * step, ny), pl.ds(h * tp, tp)]
        src = tok.at[pl.ds(h * tp, tp)] if step == 0 else slot
        return send_to(src, slot, tok_ss.at[flow, step, h], tok_rs.at[flow, step, h], on_y(sign))

    def tok_arrival(flow, step, h):
        sign = sign_of(flow)
        slot = tok_g.at[wrap(y - sign * (step + 1), ny), pl.ds(h * tp, tp)]
        return send_to(slot, slot, tok_ss.at[flow, step, h], tok_rs.at[flow, step, h], on_y(sign))

    def w_copy(flow, step, h):
        sign = sign_of(flow)
        slot = w_g.at[wrap(x - sign * step, nx), pl.ds(h * wp, wp)]
        src = w.at[pl.ds(h * wp, wp)] if step == 0 else slot
        return send_to(src, slot, w_ss.at[flow, step, h], w_rs.at[flow, step, h], on_x(sign))

    def w_arrival(flow, step, h):
        sign = sign_of(flow)
        slot = w_g.at[wrap(x - sign * (step + 1), nx), pl.ds(h * wp, wp)]
        return send_to(slot, slot, w_ss.at[flow, step, h], w_rs.at[flow, step, h], on_x(sign))

    def up_copy(i):
        return send_to(up_sel.at[wrap(x + i, nx)], up_g.at[x], up_ss.at[i], up_rs.at[i], on_x(i))

    def up_arrival(i):
        slot = up_g.at[wrap(x - i, nx)]
        return send_to(slot, slot, up_ss.at[i], up_rs.at[i], on_x(i))

    for place in range(pieces):
        for flow in (0, 1):
            order = send_order(flow, 0, ny, pieces)
            if place < len(order):
                tok_copy(flow, 0, order[place]).start()
            order = send_order(flow, 0, nx, pieces)
            if place < len(order):
                w_copy(flow, 0, order[place]).start()
        if place == 0:
            for i in range(1, nx):
                up_copy(i).start()

    def cot_copy(p):
        return send_to(cot_v.at[:, pl.ds(p * cb, cb)], cot_l.at[y_par], cot_ss.at[p], cot_rs.at[y_par], on_swap(p))

    def cot_arrival(p):
        return send_to(cot_l.at[p], cot_l.at[p], cot_ss.at[p], cot_rs.at[p], on_swap(p))

    def mag_copy(p):
        return send_to(mag_s.at[p], mag_l.at[y_par], mag_ss.at[p], mag_rs.at[y_par], on_swap(p))

    def mag_arrival(p):
        return send_to(mag_l.at[p], mag_l.at[p], mag_ss.at[p], mag_rs.at[p], on_swap(p))

    def send_cot():
        fetches[5].wait()
        for p in (0, 1):
            @pl.when(jnp.logical_not(stays[p]))
            def _():
                cot_copy(p).start()
                mag_copy(p).start()

            @pl.when(stays[p])
            def _():
                cot_l[p] = cot_v[:, p * cb:(p + 1) * cb]
                mag_l[p] = mag_s[p]

    def rank_of(block):
        rank_p[block] = dot_nt(down_sel[lax.div(block, 2)], tok_g[block])

    def squares_of(xb):
        block = w_g[xb]
        block_f32 = block.astype(F32)
        base = jnp.sum(block_f32 * block_f32, axis=0, keepdims=True)
        crossed = dot_nn(down_sel[...].reshape(s_per * RANK, kb), block)
        for c in range(s_per):
            rows = up_g[xb, c]
            quad = dot_tn(grams[c], jnp.concatenate([rows, rows, rows], axis=0))
            mixed = rows.astype(F32) * (2.0 * crossed[c * RANK:(c + 1) * RANK] + quad)
            squares = base + jnp.sum(mixed, axis=0, keepdims=True)
            ex_s[xb * s_per + c, 0:1, :] = squares[:, :hb]
            ex_s[xb * s_per + c, 1:2, :] = squares[:, hb:]

    def ex_copy(i):
        return send_to(ex_s.at[wrap(t + i, nt)], ex_l.at[t], ex_ss.at[i], ex_rs.at[i], on_t(i))

    def ex_arrival(i):
        slot = ex_l.at[wrap(t - i, nt)]
        return send_to(slot, slot, ex_ss.at[i], ex_rs.at[i], on_t(i))

    def rk_copy(i):
        return send_to(rk_s.at[lax.rem(wrap(t + i, nt), s_per)], rk_l.at[t], rk_ss.at[i], rk_rs.at[i], on_t(i))

    def rk_arrival(i):
        slot = rk_l.at[wrap(t - i, nt)]
        return send_to(slot, slot, rk_ss.at[i], rk_rs.at[i], on_t(i))

    def send_ex():
        @pl.loop(1, nt)
        def _(i):
            ex_copy(i).start()

        ex_l[t] = ex_s[t]

    def send_rk():
        for c in range(s_per):
            for p in (0, 1):
                own = rank_p[2 * c + p]
                picked = own[0:rpy]
                for y2 in range(1, ny):
                    picked = jnp.where(y == y2, own[y2 * rpy:(y2 + 1) * rpy], picked)
                rk_s[c, p * rpy:(p + 1) * rpy, :] = picked

        @pl.loop(1, nt)
        def _(i):
            rk_copy(i).start()

        rk_l[t] = rk_s[cl]

    grams = []
    for c in range(s_per):
        rows = down_sel[c]
        grams.append(jnp.concatenate(split3(dot_nt(rows, rows)), axis=0))
    fetches[0].wait()
    squares_of(x)
    fetches[4].wait()
    rank_of(y)

    events = []
    for flow in (0, 1):
        for step in range(ny // 2):
            for n, h in enumerate(send_order(flow, step, ny, pieces)):
                events.append((2.65 + 2.65 * step + 0.65 * n, 0, flow, step, h))
        for step in range(nx // 2):
            for n, h in enumerate(send_order(flow, step, nx, pieces)):
                events.append((3.3 + 5.2 * step + 1.3 * n, 1, flow, step, h))
    events.sort()
    last = {}
    for n, (_, kind, flow, step, h) in enumerate(events):
        last[kind, step] = n
    cot_at = last[0, max(ny // 2 - 2, 0)]
    for n, (_, kind, flow, step, h) in enumerate(events):
        arrival, copy, count = (tok_arrival, tok_copy, ny) if kind == 0 else (w_arrival, w_copy, nx)
        arrival(flow, step, h).wait_recv()
        if step + 1 < count // 2 and h in halves(flow, step + 1, count, pieces):
            copy(flow, step + 1, h).start()
        if n == cot_at:
            send_cot()
        if n == last[kind, step]:
            if kind == 0:
                rank_of(wrap(y + step + 1, ny))
                if step + 1 < ny // 2:
                    rank_of(wrap(y - step - 1, ny))
            else:
                if step == 0:
                    for i in range(1, nx):
                        up_arrival(i).wait_recv()
                squares_of(wrap(x + step + 1, nx))
                if step + 1 < nx // 2:
                    squares_of(wrap(x - step - 1, nx))
                if step + 1 == nx // 2:
                    send_ex()

    def stretch_tokens(c):
        return tok_g[pl.ds(2 * c, 2)].reshape(2 * tb, kb)

    def place_of(i):
        return wrap(z + half + (1 - 2 * lax.rem(i, 2)) * lax.div(i + 1, 2), nz)

    def product(slot):
        xb, c = lax.div(slot, s_per), lax.rem(slot, s_per)
        result = dot_nn(stretch_tokens(c), w_g[xb])
        for p in (0, 1):
            for j in (0, 1):
                parts[slot, 2 * p + j] = result[p * tb:(p + 1) * tb, j * hb:(j + 1) * hb]

    def sib_copy(i):
        zb = place_of(i)
        return send_to(parts.at[2 * zb + 1 - core], sib.at[zb], sib_ss.at[i], sib_rs.at[i], sibling)

    def sib_arrival(i):
        slot = sib.at[place_of(i)]
        return send_to(slot, slot, sib_ss.at[i], sib_rs.at[i], sibling)

    def products(first, end):
        @pl.loop(first, end)
        def _(i):
            product(2 * place_of(i) + 1 - core)
            sib_copy(i).start()
            product(2 * place_of(i) + core)

    def ring_copy(flow, step, q):
        sign = sign_of(flow)
        zb = wrap(z + sign * (half - step), nz)
        return send_to(
            parts.at[2 * zb + core, q], ring.at[flow, step, q],
            ring_ss.at[flow, step, q], ring_rs.at[flow, step, q], on_z(sign),
        )

    def ring_has(flow, step, q):
        return step > 0 or q // 2 == flow

    def ring_send(flow, step, q):
        zb = wrap(z + sign_of(flow) * (half - step), nz)
        value = parts[2 * zb + core, q] + sib[zb, q]
        if step > 0 and ring_has(flow, step - 1, q):
            ring_copy(flow, step - 1, q).wait_recv()
            value = value + ring[flow, step - 1, q]
        parts[2 * zb + core, q] = value
        ring_copy(flow, step, q).start()

    ring_order = ((2, 3, 0, 1), (0, 1, 2, 3))

    def ring_start():
        sib_arrival(0).wait_recv()
        for n in (2, 3):
            for flow in (0, 1):
                ring_send(flow, 0, ring_order[flow][n])

    def ring_step(step, n):
        if n == 0:
            sib_arrival(2 * step - 1).wait_recv()
            sib_arrival(2 * step).wait_recv()
        for flow in (0, 1):
            ring_send(flow, step, ring_order[flow][n])

    norms = {}

    def after_ex():
        @pl.loop(1, nt)
        def _(i):
            ex_arrival(i).wait_recv()

        for p in (0, 1):
            @pl.when(jnp.logical_not(stays[p]))
            def _():
                cot_arrival(p).wait_recv()
                mag_arrival(p).wait_recv()

        total = jnp.sum(ex_l[...], axis=0)
        squares = jnp.concatenate([total[0:1], total[1:2]], axis=1)
        norm = jnp.sqrt(squares + 1e-06)
        scaling = mag_l[0][0:1] / norm
        scaled = cot_l[...].reshape(2 * tb, cb).astype(F32) * scaling
        scaled_s[...] = scaled
        rows = up_g[xq, cl]
        parts3 = split3(scaled)
        back = dot_nt(rows, parts3[0]) + (dot_nt(rows, parts3[1]) + dot_nt(rows, parts3[2]))
        for y2 in range(ny):
            f_s[y2, 0:rpy, :] = back[y2 * rpy:(y2 + 1) * rpy, :tb]
            f_s[y2, rpy:2 * rpy, :] = back[y2 * rpy:(y2 + 1) * rpy, tb:]

        @pl.loop(1, ny)
        def _(i):
            f_copy(i).start()

        f_l[y] = f_s[y]
        norms["norm"], norms["scaling"] = norm, scaling

    def f_copy(i):
        return send_to(f_s.at[wrap(y + i, ny)], f_l.at[y], f_ss.at[i], f_rs.at[i], on_y(i))

    def f_arrival(i):
        slot = f_l.at[wrap(y - i, ny)]
        return send_to(slot, slot, f_ss.at[i], f_rs.at[i], on_y(i))

    def r_copy(i):
        return send_to(r_s, r_l.at[y], r_ss.at[i], r_rs.at[i], on_y(i))

    def r_arrival(i):
        slot = r_l.at[wrap(y - i, ny)]
        return send_to(slot, slot, r_ss.at[i], r_rs.at[i], on_y(i))

    def h_copy(i):
        return send_to(h_s, h_l.at[t], h_ss.at[i], h_rs.at[i], on_t(i))

    def h_arrival(i):
        slot = h_l.at[wrap(t - i, nt)]
        return send_to(slot, slot, h_ss.at[i], h_rs.at[i], on_t(i))

    def after_rk():
        @pl.loop(1, nt)
        def _(i):
            rk_arrival(i).wait_recv()

        r_s[...] = jnp.sum(rk_l[...], axis=0)

        @pl.loop(1, ny)
        def _(i):
            r_copy(i).start()

        r_l[y] = r_s[...]

    def after_f():
        @pl.loop(1, ny)
        def _(i):
            f_arrival(i).wait_recv()

        h_s[...] = jnp.sum(f_l[...], axis=0)

        @pl.loop(1, nt)
        def _(i):
            h_copy(i).start()

        h_l[t] = h_s[...]

    def u_copy(y2):
        return send_to(u_s, gu.at[x, cl, y_par], u_ss.at[y2], u_rs.at[cl, y_par], dev(x, y2, t_out))

    def u_arrival(c, p):
        slot = gu.at[x, c, p]
        return send_to(slot, slot, u_ss.at[0], u_rs.at[c, p], on_swap(p))

    def after_r():
        @pl.loop(1, ny)
        def _(i):
            r_arrival(i).wait_recv()

        for y2 in range(ny):
            rank_s[y2 * rpy:(y2 + 1) * rpy, :tb] = r_l[y2, 0:rpy, :]
            rank_s[y2 * rpy:(y2 + 1) * rpy, tb:] = r_l[y2, rpy:2 * rpy, :]
        a1, a2, a3 = split3(rank_s[...])
        b1, b2, b3 = split3(scaled_s[...])
        low = dot_nn(a3, b1) + dot_nn(a2, b2) + dot_nn(a1, b3)
        u_s[...] = dot_nn(a1, b1) + (dot_nn(a2, b1) + dot_nn(a1, b2) + low)

        @pl.loop(0, ny)
        def _(y2):
            @pl.when(jnp.logical_not(jnp.logical_and(at_home, y2 == y)))
            def _():
                u_copy(y2).start()

        @pl.when(at_home)
        def _():
            gu[x, cl, y_par] = u_s[...]

        rows = up_g[xq, cl]
        low_s[...] = dot_tn(
            jnp.concatenate([a1, a2, a3], axis=0), jnp.concatenate([rows, rows, rows], axis=0)
        )

    def ux_copy(flow, step, h):
        slot = gu.at[wrap(x - sign_of(flow) * step, nx), pl.ds(h * (s_per // 2), s_per // 2)]
        return send_to(slot, slot, ux_ss.at[flow, step, h], ux_rs.at[flow, step, h], on_x(sign_of(flow)))

    def ux_arrival(flow, step, h):
        slot = gu.at[wrap(x - sign_of(flow) * (step + 1), nx), pl.ds(h * (s_per // 2), s_per // 2)]
        return send_to(slot, slot, ux_ss.at[flow, step, h], ux_rs.at[flow, step, h], on_x(sign_of(flow)))

    def dx_copy(flow, step, h):
        slot = gd.at[wrap(x - sign_of(flow) * step, nx), pl.ds(h * (ny // 2), ny // 2)]
        return send_to(slot, slot, dx_ss.at[flow, step, h], dx_rs.at[flow, step, h], on_x(sign_of(flow)))

    def dx_arrival(flow, step, h):
        slot = gd.at[wrap(x - sign_of(flow) * (step + 1), nx), pl.ds(h * (ny // 2), ny // 2)]
        return send_to(slot, slot, dx_ss.at[flow, step, h], dx_rs.at[flow, step, h], on_x(sign_of(flow)))

    def start_x(copy):
        for n in (0, 1):
            for flow in (0, 1):
                order = send_order(flow, 0, nx, 2)
                if n < len(order):
                    copy(flow, 0, order[n]).start()

    def pass_x(copy, arrival, step):
        if step >= nx // 2:
            return
        for n in (0, 1):
            for flow in (0, 1):
                order = send_order(flow, step, nx, 2)
                if n < len(order):
                    arrival(flow, step, order[n]).wait_recv()
                    if step + 1 < nx // 2 and order[n] in halves(flow, step + 1, nx, 2):
                        copy(flow, step + 1, order[n]).start()

    def after_u():
        @pl.loop(0, ny)
        def _(i):
            c, p = lax.div(i, 2), lax.rem(i, 2)

            @pl.when(jnp.logical_not(jnp.logical_and(at_home, i == y)))
            def _():
                u_arrival(c, p).wait_recv()

        start_x(ux_copy)

    def dy_copy(i):
        slot = gd.at[x, y]
        return send_to(slot, slot, dy_ss.at[i], dy_rs.at[i], on_y(i))

    def dy_arrival(i):
        slot = gd.at[x, wrap(y - i, ny)]
        return send_to(slot, slot, dy_ss.at[i], dy_rs.at[i], on_y(i))

    def after_h():
        @pl.loop(1, nt)
        def _(i):
            h_arrival(i).wait_recv()

        for c in range(s_per):
            tile = h_l[c]
            for xb in range(1, nx):
                tile = tile + h_l[xb * s_per + c]
            tile = jnp.concatenate([tile, jnp.zeros((8 - 2 * rpy, tb), F32)], axis=0) if rpy < 4 else tile
            stacked = jnp.concatenate([v.astype(F32) for v in split3(tile)] + [jnp.zeros_like(tile)], axis=0)
            stacked = stacked.astype(BF16)
            both = []
            for p in (0, 1):
                full = dot_nn(stacked, tok_g[2 * c + p])
                both.append(full[0:8] + (full[8:16] + full[16:24]))
            gd[x, y, c * rpy:(c + 1) * rpy, :] = both[0][0:rpy] + both[1][rpy:2 * rpy]

        @pl.loop(1, ny)
        def _(i):
            dy_copy(i).start()

    def after_dy():
        @pl.loop(1, ny)
        def _(i):
            dy_arrival(i).wait_recv()

        start_x(dx_copy)

    products(0, min(3, nz))
    send_rk()
    after_ex()
    ring_start()
    plan = []
    if half > 1:
        plan += [(0.1, lambda: ring_step(1, 0)), (0.2, lambda: ring_step(1, 1))]
        plan += [(3.3, lambda: ring_step(1, 2)), (4.6, lambda: ring_step(1, 3))]
    for step in range(2, half):
        for n in range(4):
            plan.append((5.9 + 5.2 * (step - 2) + 1.3 * n, functools.partial(ring_step, step, n)))
    plan += [
        (0.3, lambda: products(min(3, nz), nz)),
        (2.2, after_rk),
        (3.0, after_f),
        (4.0, after_r),
        (6.0, after_h),
        (8.4, after_u),
        (10.6, after_dy),
        (13.0, lambda: pass_x(ux_copy, ux_arrival, 0)),
        (15.2, lambda: pass_x(dx_copy, dx_arrival, 0)),
        (16.5, lambda: pass_x(ux_copy, ux_arrival, 1)),
    ]
    plan.sort(key=lambda item: item[0])
    for _, action in plan:
        action()
    gu_write = pltpu.make_async_copy(gu, gu_out, out_s.at[0])
    gu_write.start()

    norm, scaling = norms["norm"], norms["scaling"]

    def pr_copy(p, j):
        return send_to(proj_s.at[p, j], proj_l.at[y_par, j], pr_ss.at[p, j], pr_rs.at[y_par, j], on_swap(p))

    def pr_arrival(p, j):
        return send_to(proj_l.at[p, j], proj_l.at[p, j], pr_ss.at[p, j], pr_rs.at[p, j], on_swap(p))

    sib_arrival(nz - 1).wait_recv()
    mag_sum = [None, None]
    for n in range(4):
        for flow in (0, 1):
            q = ring_order[flow][n]
            if ring_has(flow, half - 1, q):
                ring_copy(flow, half - 1, q).wait_recv()
        for q in ([0, 2] if n == 2 else [1, 3] if n == 3 else []):
            p, j = q // 2, q % 2
            lanes = slice(j * hb, (j + 1) * hb)
            value = parts[t, q] + sib[z, q]
            for flow in (0, 1):
                if ring_has(flow, half - 1, q):
                    value = value + ring[flow, half - 1, q]
            value = value + low_s[p * tb:(p + 1) * tb, lanes]
            proj_s[p, j] = (value * scaling[:, lanes]).astype(BF16)

            @pl.when(jnp.logical_not(stays[p]))
            def _():
                pr_copy(p, j).start()

            @pl.when(stays[p])
            def _():
                proj_l[p, j] = proj_s[p, j]

            term = jnp.sum(cot_l[p, :, lanes].astype(F32) * value, axis=0, keepdims=True)
            mag_sum[j] = term if mag_sum[j] is None else mag_sum[j] + term

    for j in (0, 1):
        m_s[j:j + 1, :] = mag_sum[j] / norm[:, j * hb:(j + 1) * hb]

    def m_copy(i):
        return send_to(m_s, m_g.at[x, cl, y_par], m_ss.at[i], m_rs.at[x, cl, y_par], target(i))

    def m_arrival(i):
        xb, rest = lax.div(i, ny), lax.rem(i, ny)
        c, p = lax.div(rest, 2), lax.rem(rest, 2)
        slot = m_g.at[xb, c, p]
        return send_to(slot, slot, m_ss.at[i], m_rs.at[xb, c, p], target(i))

    def not_self(i):
        return jnp.logical_not(jnp.logical_and(at_home, i == dp))

    @pl.loop(0, outs)
    def _(i):
        @pl.when(not_self(i))
        def _():
            m_copy(i).start()

    @pl.when(at_home)
    def _():
        m_g[x, cl, y_par] = m_s[...]

    pass_x(dx_copy, dx_arrival, 1)
    gd_write = pltpu.make_async_copy(gd, gd_out, out_s.at[1])
    gd_write.start()

    def proj_write(p, j):
        return pltpu.make_async_copy(
            proj_l.at[p, j], proj_out.at[:, pl.ds(p * cb + j * hb, hb)], out_s.at[2 + 2 * p + j]
        )

    for flow in (0, 1):
        for step in range(ny // 2):
            for h in halves(flow, step, ny, pieces):
                tok_copy(flow, step, h).wait_send()
        for step in range(nx // 2):
            for h in halves(flow, step, nx, pieces):
                w_copy(flow, step, h).wait_send()
            for h in halves(flow, step, nx, 2):
                ux_copy(flow, step, h).wait_send()
                dx_copy(flow, step, h).wait_send()
        for step in range(half):
            for q in range(4):
                if ring_has(flow, step, q):
                    ring_copy(flow, step, q).wait_send()

    @pl.loop(1, nt)
    def _(i):
        ex_copy(i).wait_send()
        rk_copy(i).wait_send()
        h_copy(i).wait_send()

    @pl.loop(0, nz)
    def _(i):
        sib_copy(i).wait_send()

    @pl.loop(1, ny)
    def _(i):
        f_copy(i).wait_send()
        r_copy(i).wait_send()
        dy_copy(i).wait_send()

    @pl.loop(0, ny)
    def _(y2):
        @pl.when(jnp.logical_not(jnp.logical_and(at_home, y2 == y)))
        def _():
            u_copy(y2).wait_send()

    for i in range(1, nx):
        up_copy(i).wait_send()
    for p in (0, 1):
        @pl.when(jnp.logical_not(stays[p]))
        def _():
            cot_copy(p).wait_send()
            mag_copy(p).wait_send()

    for p in (0, 1):
        for j in (0, 1):
            @pl.when(jnp.logical_not(stays[p]))
            def _():
                pr_arrival(p, j).wait_recv()
                pr_copy(p, j).wait_send()

            proj_write(p, j).start()

    @pl.loop(0, outs)
    def _(i):
        @pl.when(not_self(i))
        def _():
            m_arrival(i).wait_recv()
            m_copy(i).wait_send()

    m_write = pltpu.make_async_copy(m_g, m_out, out_s.at[6])
    m_write.start()
    gu_write.wait()
    gd_write.wait()
    for p in (0, 1):
        for j in (0, 1):
            proj_write(p, j).wait()
    m_write.wait()


def scatter_kernel(nx, ny, tenant, proj, gu_in, gd_in, m_in, proj_out, down_out, up_out, mag_out, gu, gd, m, sems):
    s_per = ny // 2
    rpy = RANK // ny
    copies = [
        pltpu.make_async_copy(src, dst, sems.at[n])
        for n, (src, dst) in enumerate(((gu_in, gu), (gd_in, gd), (m_in, m), (proj, proj_out)))
    ]
    for copy in copies:
        copy.start()
    down_out[...] = jnp.zeros_like(down_out)
    up_out[...] = jnp.zeros_like(up_out)
    for copy in copies:
        copy.wait()
    hb = m.shape[4]
    row_ids = lax.broadcasted_iota(jnp.int32, (mag_out.shape[0], hb), 0)
    mag_sums = [jnp.zeros(row_ids.shape, F32)] * 4
    for xb in range(nx):
        for c in range(s_per):
            who = tenant[xb * s_per + c]
            for p in (0, 1):
                up_out[who, :, 2 * hb * p:2 * hb * (p + 1)] += gu[xb, c, p]
                for j in (0, 1):
                    row = m[xb, c, p, j:j + 1, :]
                    mag_sums[2 * p + j] = mag_sums[2 * p + j] + jnp.where(row_ids == who, row, 0.0)
            rows = [gd[xb, yb, c * rpy:(c + 1) * rpy, :] for yb in range(ny)]
            down_out[who] += jnp.concatenate(rows, axis=0)
    for q in range(4):
        mag_out[:, hb * q:hb * (q + 1)] = mag_sums[q]


def per_device(nx, ny, nt, tokens, base_weight, adapter_down, adapter_up, magnitude, tenant, cotangent):
    tb, kb = tokens.shape
    cb = base_weight.shape[1]
    hb = cb // 2
    tenants = adapter_down.shape[0]
    s_per = ny // 2
    nz = nt // 2
    rpy = RANK // ny
    dma = pltpu.SemaphoreType.DMA
    vmem = pl.BlockSpec(memory_space=pltpu.VMEM)
    smem = pl.BlockSpec(memory_space=pltpu.SMEM)
    hbm = pl.BlockSpec(memory_space=pltpu.HBM)
    scratch = [
        pltpu.VMEM(adapter_down.shape, BF16),
        pltpu.VMEM(adapter_up.shape, BF16),
        pltpu.VMEM(magnitude.shape, F32),
        pltpu.VMEM(cotangent.shape, BF16),
        pltpu.VMEM((ny, tb, kb), BF16),
        pltpu.VMEM((nx, kb, cb), BF16),
        pltpu.VMEM((nx, s_per, RANK, cb), BF16),
        pltpu.VMEM((nx, s_per, RANK, cb), BF16),
        pltpu.VMEM((s_per, RANK, kb), BF16),
        pltpu.VMEM((2, tb, cb), BF16),
        pltpu.VMEM((2, 8, cb), F32),
        pltpu.VMEM((2, 8, cb), F32),
        pltpu.VMEM((nt, 2, hb), F32),
        pltpu.VMEM((nt, 2, hb), F32),
        pltpu.VMEM((s_per, 2 * rpy, tb), F32),
        pltpu.VMEM((nt, 2 * rpy, tb), F32),
        pltpu.VMEM((ny, RANK, tb), F32),
        pltpu.VMEM((nt, 4, tb, hb), F32),
        pltpu.VMEM((nz, 4, tb, hb), F32),
        pltpu.VMEM((2, nz // 2, 4, tb, hb), F32),
        pltpu.VMEM((2 * tb, cb), F32),
        pltpu.VMEM((ny, 2 * rpy, tb), F32),
        pltpu.VMEM((ny, 2 * rpy, tb), F32),
        pltpu.VMEM((2 * rpy, tb), F32),
        pltpu.VMEM((ny, 2 * rpy, tb), F32),
        pltpu.VMEM((2 * rpy, tb), F32),
        pltpu.VMEM((nt, 2 * rpy, tb), F32),
        pltpu.VMEM((RANK, 2 * tb), F32),
        pltpu.VMEM((RANK, cb), F32),
        pltpu.VMEM((nx, s_per, 2, RANK, cb), F32),
        pltpu.VMEM((nx, ny, s_per * rpy, kb), F32),
        pltpu.VMEM((2 * tb, cb), F32),
        pltpu.VMEM((2, 2, tb, hb), BF16),
        pltpu.VMEM((2, 2, tb, hb), BF16),
        pltpu.VMEM((2, hb), F32),
        pltpu.VMEM((nx, s_per, 2, 2, hb), F32),
        dma((6,)),
    ]
    pairs = [
        ((2, ny // 2, 4),) * 2, ((2, nx // 2, 4),) * 2, ((nx,),) * 2, ((2,),) * 2, ((2,),) * 2,
        ((nt,),) * 2, ((nt,),) * 2, ((nz,),) * 2, ((2, nz // 2, 4),) * 2,
        ((ny,),) * 2, ((ny,),) * 2, ((nt,),) * 2,
        ((ny,), (s_per, 2)), ((2, nx // 2, 2),) * 2, ((ny,),) * 2, ((2, nx // 2, 2),) * 2,
        ((2, 2),) * 2, ((nx * ny,), (nx, s_per, 2)),
    ]
    for first, second in pairs:
        scratch += [dma(first), dma(second)]
    scratch.append(dma((7,)))
    proj, up_terms, down_terms, mags = pl.pallas_call(
        functools.partial(exchange_kernel, nx, ny, nt),
        out_shape=(
            jax.ShapeDtypeStruct((tb, 2 * cb), BF16),
            jax.ShapeDtypeStruct((nx, s_per, 2, RANK, cb), F32),
            jax.ShapeDtypeStruct((nx, ny, s_per * rpy, kb), F32),
            jax.ShapeDtypeStruct((nx, s_per, 2, 2, hb), F32),
        ),
        in_specs=[smem] + [hbm] * 6,
        out_specs=(hbm,) * 4,
        scratch_shapes=scratch,
        compiler_params=pltpu.CompilerParams(
            collective_id=0, has_side_effects=True, vmem_limit_bytes=60 * 1024 * 1024
        ),
        name="exchange",
    )(tenant, tokens, base_weight, adapter_down, adapter_up, magnitude, cotangent)
    return pl.pallas_call(
        functools.partial(scatter_kernel, nx, ny),
        out_shape=(
            jax.ShapeDtypeStruct((tb, 2 * cb), BF16),
            jax.ShapeDtypeStruct((tenants, RANK, kb), F32),
            jax.ShapeDtypeStruct((tenants, RANK, 2 * cb), F32),
            jax.ShapeDtypeStruct((tenants, 2 * cb), F32),
        ),
        in_specs=[smem] + [hbm] * 4,
        out_specs=(hbm, vmem, vmem, vmem),
        scratch_shapes=[
            pltpu.VMEM(up_terms.shape, F32),
            pltpu.VMEM(down_terms.shape, F32),
            pltpu.VMEM(mags.shape, F32),
            dma((4,)),
        ],
        compiler_params=pltpu.CompilerParams(vmem_limit_bytes=60 * 1024 * 1024),
        name="scatter",
    )(tenant, proj, up_terms, down_terms, mags)


def solution(mesh, nx=X_CHIPS):
    ny = mesh.shape["dp"] // nx
    nt = mesh.shape["tensor"]
    in_specs = (
        P("dp", "tensor"),
        P("tensor", "dp"),
        P(None, None, "tensor"),
        P(None, None, "dp"),
        P(None, "tensor"),
        P(),
        P("dp", "tensor"),
    )
    out_specs = (
        P("dp", "tensor"),
        P(None, None, "tensor"),
        P(None, None, "tensor"),
        P(None, "tensor"),
    )
    return jax.shard_map(
        functools.partial(per_device, nx, ny, nt),
        mesh=mesh, in_specs=in_specs, out_specs=out_specs, check_vma=False,
    )
```

time: 432 us -> 84.7 us (0.20)
  waiting for transfers between devices: 280 us -> 0 us
  blocking collectives: 94.8 us -> 0 us
  Pallas kernels: 0 us -> 83.9 us
  matrix products: 16.2 us -> 0 us
  between operations: 15.9 us -> 0.64 us
  other arithmetic: 9.96 us -> 0 us
  local copies, waits for them, and re-layouts: 7.48 us -> 0 us
  starting transfers between devices: 5.06 us -> 0 us
    psum x1 -> x0, waiting for transfers between devices: 159 us -> none  [per_device(): lax.psum((dense_down, dense_up, dense_mag), 'dp')]
    all_gather x1 -> x0, waiting for transfers between devices: 115 us -> none  [per_device(): weight_full = lax.all_gather(base_weight, 'dp', axis=1, tiled=True)]
    psum x2 -> x0, blocking collectives: 94.8 us -> none  [per_device(): rank_acts, squares = lax.psum((rank_part, square_part), 'tensor')]
    pallas_call x0 -> x2, Pallas kernels: none -> 83.9 us  [the longest x1 76.6 us: per_device(): pl.pallas_call(functools.partial(exchange_kernel, nx, ny, nt), out_shape=...]
    dot_general x9 -> x0, matrix products: 16.2 us -> none  [the longest x1 6.7 us: per_device(): jnp.dot(tokens, weight_full, preferred_element_type=jnp.float32)]
    unnamed x12 -> x0, local copies, waits for them, and re-layouts: 6.12 us -> none
    reduce_sum x2 -> x0, other arithmetic: 5.5 us -> none  [the longest x1 5.41 us: norm_terms(): base_squares = jnp.sum(jnp.square(weight_rows.astype(jnp.float32)), axis=0)]
    all_to_all x1 -> x0, starting transfers between devices: 4.94 us -> none  [per_device(): lax.all_to_all(up_selected, 'dp', split_axis=0, concat_axis=3, tiled=True)]
  transfers between devices with their start and end apart: 4 -> 0, of which waited for: 3 -> 0; matrix products, arithmetic and copies ran while one was open for 4% -> 0% of each run, Pallas kernels for 0% -> 0%
where the time goes in v2:
time: 84.7 us; the launch traced here: 84.5 us
  Pallas kernels  83.9 us (99%)
    pallas_call x1, Pallas kernels, per_device(): pl.pallas_call(functools.partial(exchange_kernel, nx, ny, nt), out_shape=...  76.6 us
    pallas_call x1, Pallas kernels, per_device(): pl.pallas_call(functools.partial(scatter_kernel, nx, ny), out_shape=(jax....  7.23 us

profile of v2, /device:TPU:1, one launch (start us, length us, event | category | flops | bytes accessed | tf_op | source)
XLA Modules:
  0.0 84.5 jit_solution(13995580084330953245)
XLA Ops:
  0.6 76.6 %exchange.1 = (bf16[128,512]{1,0:T(8,128)(2,1)}, f32[4,4,2,16,256]{4,3,2,1,0:T(8,128)}, f32[4,8,8,512]{3,2,1,0:T(8,128)}, f32[4,4,2,2,128]{4,3,2,1,0:T(2,128)}) custom-call(s32[16]{0:T(128)} %tenant.3, bf16[128,512]{1,0:T(8,128)(2,1)} %tok.1, bf16[512,256]{1,0:T(8,128)(2,1)} %w.1, bf16[32,16,512]{2,1,0:T(8,128)(2,1)} %down.1, bf16[32,16,256]{2,1,0:T(8,128)(2,1)} %up.1, ...), custom_call_target="tpu_custom_call" | custom-call | tf_op jit(solution)/shard_map/exchange/pallas_call | solution.py:865
  77.3 7.2 %scatter.1 = (bf16[128,512]{1,0:T(8,128)(2,1)}, f32[32,16,512]{2,1,0:T(8,128)}, f32[32,16,512]{2,1,0:T(8,128)}, f32[32,512]{1,0:T(8,128)}) custom-call(s32[16]{0:T(128)} %tenant.3, bf16[128,512]{1,0:T(8,128)(2,1)} %get-tuple-element.8.proj, f32[4,4,2,16,256]{4,3,2,1,0:T(8,128)} %get-tuple-element.9.gu_in, f32[4,8,8,512]{3,2,1,0:T(8,128)} %get-tuple-element.10.gd_in, ...), custom_call_target="tpu_custom_call" | custom-call | tf_op jit(solution)/shard_map/scatter/pallas_call | solution.py:881

commit v3 on v2

--- a/solution.py
+++ b/solution.py
@@ -59,9 +59,9 @@
 
 def exchange_kernel(
     nx, ny, nt,
-    tenant, tok, w, down, up, mag, cot,
+    tenant_in, tok, w, down, up, mag, cot,
     proj_out, gu_out, gd_out, m_out,
-    down_v, up_v, mag_v, cot_v, tok_g, w_g, up_sel, up_g, down_sel, cot_l, mag_s, mag_l,
+    tenant, down_v, up_v, mag_v, cot_v, tok_g, w_g, up_sel, up_g, down_sel, cot_l, mag_s, mag_l,
     ex_s, ex_l, rk_s, rk_l, rank_p, parts, sib, ring,
     scaled_s, f_s, f_l, r_s, r_l, h_s, h_l, rank_s, u_s, gu, gd, low_s, proj_s, proj_l, m_s, m_g,
     in_s, tok_ss, tok_rs, w_ss, w_rs, up_ss, up_rs, cot_ss, cot_rs, mag_ss, mag_rs,
@@ -113,6 +113,7 @@
         pltpu.make_async_copy(src, dst, in_s.at[n])
         for n, (src, dst) in enumerate((
             (w, w_g.at[x]), (up, up_v), (down, down_v), (mag, mag_v), (tok, tok_g.at[y]), (cot, cot_v),
+            (tenant_in, tenant),
         ))
     ]
     for fetch in fetches:
@@ -136,23 +137,20 @@
 
     outs = nx * ny
 
-    def source(i):
-        xb, rest = lax.div(i, ny), lax.rem(i, ny)
-        return dev(xb, 2 * cl + lax.rem(rest, 2), s_per * xq + lax.div(rest, 2))
-
-    own_source = x * ny + 2 * cl + y_par
-
     def target(i):
         return (i, t_out)
 
-    @pl.loop(0, outs)
-    def _(i):
-        @pl.when(jnp.logical_not(jnp.logical_and(at_home, i == own_source)))
-        def _():
-            greet(source(i))
-
-    for fetch in fetches[1:4]:
-        fetch.wait()
+    for xb in range(nx):
+        for c in range(s_per):
+            for p in (0, 1):
+                maker = dev(xb, 2 * cl + p, s_per * xq + c)
+
+                @pl.when(jnp.logical_not(jnp.logical_and(maker[0] == dp, maker[1] == t)))
+                def _():
+                    greet(maker)
+
+    for n in (6, 1, 2, 3):
+        fetches[n].wait()
     for c in range(nx * s_per):
         up_sel[c // s_per, c % s_per] = up_v[tenant[c]]
     up_g[x] = up_sel[x]
@@ -179,34 +177,39 @@
     def sign_of(flow):
         return 1 if flow == 0 else -1
 
+    def at(count, many, flow, step, h):
+        before = sum(len(halves(flow, k, count, many)) for k in range(step))
+        place = halves(flow, step, count, many).index(h)
+        return flow * (count - 1) * many // 2 + before + place
+
     def tok_copy(flow, step, h):
         sign = sign_of(flow)
         slot = tok_g.at[wrap(y - sign * step, ny), pl.ds(h * tp, tp)]
         src = tok.at[pl.ds(h * tp, tp)] if step == 0 else slot
-        return send_to(src, slot, tok_ss.at[flow, step, h], tok_rs.at[flow, step, h], on_y(sign))
+        return send_to(src, slot, tok_ss, tok_rs.at[at(ny, pieces, flow, step, h)], on_y(sign))
 
     def tok_arrival(flow, step, h):
         sign = sign_of(flow)
         slot = tok_g.at[wrap(y - sign * (step + 1), ny), pl.ds(h * tp, tp)]
-        return send_to(slot, slot, tok_ss.at[flow, step, h], tok_rs.at[flow, step, h], on_y(sign))
+        return send_to(slot, slot, tok_ss, tok_rs.at[at(ny, pieces, flow, step, h)], on_y(sign))
 
     def w_copy(flow, step, h):
         sign = sign_of(flow)
         slot = w_g.at[wrap(x - sign * step, nx), pl.ds(h * wp, wp)]
         src = w.at[pl.ds(h * wp, wp)] if step == 0 else slot
-        return send_to(src, slot, w_ss.at[flow, step, h], w_rs.at[flow, step, h], on_x(sign))
+        return send_to(src, slot, w_ss, w_rs.at[at(nx, pieces, flow, step, h)], on_x(sign))
 
     def w_arrival(flow, step, h):
         sign = sign_of(flow)
         slot = w_g.at[wrap(x - sign * (step + 1), nx), pl.ds(h * wp, wp)]
-        return send_to(slot, slot, w_ss.at[flow, step, h], w_rs.at[flow, step, h], on_x(sign))
+        return send_to(slot, slot, w_ss, w_rs.at[at(nx, pieces, flow, step, h)], on_x(sign))
 
     def up_copy(i):
-        return send_to(up_sel.at[wrap(x + i, nx)], up_g.at[x], up_ss.at[i], up_rs.at[i], on_x(i))
-
-    def up_arrival(i):
-        slot = up_g.at[wrap(x - i, nx)]
-        return send_to(slot, slot, up_ss.at[i], up_rs.at[i], on_x(i))
+        return send_to(up_sel.at[wrap(x + i, nx)], up_g.at[x], up_ss, up_rs, on_x(i))
+
+    def up_all():
+        slots = up_g.at[pl.ds(0, nx - 1)]
+        return send_to(slots, slots, up_ss, up_rs, on_x(1))
 
     for place in range(pieces):
         for flow in (0, 1):
@@ -262,18 +265,18 @@
             ex_s[xb * s_per + c, 1:2, :] = squares[:, hb:]
 
     def ex_copy(i):
-        return send_to(ex_s.at[wrap(t + i, nt)], ex_l.at[t], ex_ss.at[i], ex_rs.at[i], on_t(i))
-
-    def ex_arrival(i):
-        slot = ex_l.at[wrap(t - i, nt)]
-        return send_to(slot, slot, ex_ss.at[i], ex_rs.at[i], on_t(i))
+        return send_to(ex_s.at[wrap(t + i, nt)], ex_l.at[t], ex_ss, ex_rs, on_t(i))
+
+    def ex_all():
+        slots = ex_l.at[pl.ds(0, nt - 1)]
+        return send_to(slots, slots, ex_ss, ex_rs, on_t(1))
 
     def rk_copy(i):
-        return send_to(rk_s.at[lax.rem(wrap(t + i, nt), s_per)], rk_l.at[t], rk_ss.at[i], rk_rs.at[i], on_t(i))
-
-    def rk_arrival(i):
-        slot = rk_l.at[wrap(t - i, nt)]
-        return send_to(slot, slot, rk_ss.at[i], rk_rs.at[i], on_t(i))
+        return send_to(rk_s.at[lax.rem(wrap(t + i, nt), s_per)], rk_l.at[t], rk_ss, rk_rs, on_t(i))
+
+    def rk_all():
+        slots = rk_l.at[pl.ds(0, nt - 1)]
+        return send_to(slots, slots, rk_ss, rk_rs, on_t(1))
 
     def send_ex():
         @pl.loop(1, nt)
@@ -333,8 +336,7 @@
                     rank_of(wrap(y - step - 1, ny))
             else:
                 if step == 0:
-                    for i in range(1, nx):
-                        up_arrival(i).wait_recv()
+                    up_all().wait_recv()
                 squares_of(wrap(x + step + 1, nx))
                 if step + 1 < nx // 2:
                     squares_of(wrap(x - step - 1, nx))
@@ -356,11 +358,11 @@
 
     def sib_copy(i):
         zb = place_of(i)
-        return send_to(parts.at[2 * zb + 1 - core], sib.at[zb], sib_ss.at[i], sib_rs.at[i], sibling)
+        return send_to(parts.at[2 * zb + 1 - core], sib.at[zb], sib_ss, sib_rs.at[i], sibling)
 
     def sib_arrival(i):
         slot = sib.at[place_of(i)]
-        return send_to(slot, slot, sib_ss.at[i], sib_rs.at[i], sibling)
+        return send_to(slot, slot, sib_ss, sib_rs.at[i], sibling)
 
     def products(first, end):
         @pl.loop(first, end)
@@ -369,12 +371,15 @@
             sib_copy(i).start()
             product(2 * place_of(i) + core)
 
+    def ring_at(flow, step, q):
+        return flow * (nz - 1) * 2 + (q % 2 if step == 0 else 2 + 4 * (step - 1) + q)
+
     def ring_copy(flow, step, q):
         sign = sign_of(flow)
         zb = wrap(z + sign * (half - step), nz)
         return send_to(
             parts.at[2 * zb + core, q], ring.at[flow, step, q],
-            ring_ss.at[flow, step, q], ring_rs.at[flow, step, q], on_z(sign),
+            ring_ss, ring_rs.at[ring_at(flow, step, q)], on_z(sign),
         )
 
     def ring_has(flow, step, q):
@@ -407,9 +412,7 @@
     norms = {}
 
     def after_ex():
-        @pl.loop(1, nt)
-        def _(i):
-            ex_arrival(i).wait_recv()
+        ex_all().wait_recv()
 
         for p in (0, 1):
             @pl.when(jnp.logical_not(stays[p]))
@@ -438,30 +441,28 @@
         norms["norm"], norms["scaling"] = norm, scaling
 
     def f_copy(i):
-        return send_to(f_s.at[wrap(y + i, ny)], f_l.at[y], f_ss.at[i], f_rs.at[i], on_y(i))
-
-    def f_arrival(i):
-        slot = f_l.at[wrap(y - i, ny)]
-        return send_to(slot, slot, f_ss.at[i], f_rs.at[i], on_y(i))
+        return send_to(f_s.at[wrap(y + i, ny)], f_l.at[y], f_ss, f_rs, on_y(i))
+
+    def f_all():
+        slots = f_l.at[pl.ds(0, ny - 1)]
+        return send_to(slots, slots, f_ss, f_rs, on_y(1))
 
     def r_copy(i):
-        return send_to(r_s, r_l.at[y], r_ss.at[i], r_rs.at[i], on_y(i))
-
-    def r_arrival(i):
-        slot = r_l.at[wrap(y - i, ny)]
-        return send_to(slot, slot, r_ss.at[i], r_rs.at[i], on_y(i))
+        return send_to(r_s, r_l.at[y], r_ss, r_rs, on_y(i))
+
+    def r_all():
+        slots = r_l.at[pl.ds(0, ny - 1)]
+        return send_to(slots, slots, r_ss, r_rs, on_y(1))
 
     def h_copy(i):
-        return send_to(h_s, h_l.at[t], h_ss.at[i], h_rs.at[i], on_t(i))
-
-    def h_arrival(i):
-        slot = h_l.at[wrap(t - i, nt)]
-        return send_to(slot, slot, h_ss.at[i], h_rs.at[i], on_t(i))
+        return send_to(h_s, h_l.at[t], h_ss, h_rs, on_t(i))
+
+    def h_all():
+        slots = h_l.at[pl.ds(0, nt - 1)]
+        return send_to(slots, slots, h_ss, h_rs, on_t(1))
 
     def after_rk():
-        @pl.loop(1, nt)
-        def _(i):
-            rk_arrival(i).wait_recv()
+        rk_all().wait_recv()
 
         r_s[...] = jnp.sum(rk_l[...], axis=0)
 
@@ -472,9 +473,7 @@
         r_l[y] = r_s[...]
 
     def after_f():
-        @pl.loop(1, ny)
-        def _(i):
-            f_arrival(i).wait_recv()
+        f_all().wait_recv()
 
         h_s[...] = jnp.sum(f_l[...], axis=0)
 
@@ -485,16 +484,23 @@
         h_l[t] = h_s[...]
 
     def u_copy(y2):
-        return send_to(u_s, gu.at[x, cl, y_par], u_ss.at[y2], u_rs.at[cl, y_par], dev(x, y2, t_out))
-
-    def u_arrival(c, p):
-        slot = gu.at[x, c, p]
-        return send_to(slot, slot, u_ss.at[0], u_rs.at[c, p], on_swap(p))
+        return send_to(u_s, gu.at[x, 2 * cl + y_par], u_ss, u_rs, dev(x, y2, t_out))
+
+    def u_all(count):
+        slots = gu.at[x, pl.ds(0, count)]
+        return send_to(slots, slots, u_ss, u_rs, on_x(1))
+
+    def by_home(wait, count):
+        @pl.when(at_home)
+        def _():
+            wait(count - 1)
+
+        @pl.when(away)
+        def _():
+            wait(count)
 
     def after_r():
-        @pl.loop(1, ny)
-        def _(i):
-            r_arrival(i).wait_recv()
+        r_all().wait_recv()
 
         for y2 in range(ny):
             rank_s[y2 * rpy:(y2 + 1) * rpy, :tb] = r_l[y2, 0:rpy, :]
@@ -512,7 +518,7 @@
 
         @pl.when(at_home)
         def _():
-            gu[x, cl, y_par] = u_s[...]
+            gu[x, 2 * cl + y_par] = u_s[...]
 
         rows = up_g[xq, cl]
         low_s[...] = dot_tn(
@@ -520,20 +526,20 @@
         )
 
     def ux_copy(flow, step, h):
-        slot = gu.at[wrap(x - sign_of(flow) * step, nx), pl.ds(h * (s_per // 2), s_per // 2)]
-        return send_to(slot, slot, ux_ss.at[flow, step, h], ux_rs.at[flow, step, h], on_x(sign_of(flow)))
+        slot = gu.at[wrap(x - sign_of(flow) * step, nx), pl.ds(h * (ny // 2), ny // 2)]
+        return send_to(slot, slot, ux_ss, ux_rs.at[at(nx, 2, flow, step, h)], on_x(sign_of(flow)))
 
     def ux_arrival(flow, step, h):
-        slot = gu.at[wrap(x - sign_of(flow) * (step + 1), nx), pl.ds(h * (s_per // 2), s_per // 2)]
-        return send_to(slot, slot, ux_ss.at[flow, step, h], ux_rs.at[flow, step, h], on_x(sign_of(flow)))
+        slot = gu.at[wrap(x - sign_of(flow) * (step + 1), nx), pl.ds(h * (ny // 2), ny // 2)]
+        return send_to(slot, slot, ux_ss, ux_rs.at[at(nx, 2, flow, step, h)], on_x(sign_of(flow)))
 
     def dx_copy(flow, step, h):
         slot = gd.at[wrap(x - sign_of(flow) * step, nx), pl.ds(h * (ny // 2), ny // 2)]
-        return send_to(slot, slot, dx_ss.at[flow, step, h], dx_rs.at[flow, step, h], on_x(sign_of(flow)))
+        return send_to(slot, slot, dx_ss, dx_rs.at[at(nx, 2, flow, step, h)], on_x(sign_of(flow)))
 
     def dx_arrival(flow, step, h):
         slot = gd.at[wrap(x - sign_of(flow) * (step + 1), nx), pl.ds(h * (ny // 2), ny // 2)]
-        return send_to(slot, slot, dx_ss.at[flow, step, h], dx_rs.at[flow, step, h], on_x(sign_of(flow)))
+        return send_to(slot, slot, dx_ss, dx_rs.at[at(nx, 2, flow, step, h)], on_x(sign_of(flow)))
 
     def start_x(copy):
         for n in (0, 1):
@@ -554,28 +560,19 @@
                         copy(flow, step + 1, order[n]).start()
 
     def after_u():
-        @pl.loop(0, ny)
-        def _(i):
-            c, p = lax.div(i, 2), lax.rem(i, 2)
-
-            @pl.when(jnp.logical_not(jnp.logical_and(at_home, i == y)))
-            def _():
-                u_arrival(c, p).wait_recv()
-
+        by_home(lambda count: u_all(count).wait_recv(), ny)
         start_x(ux_copy)
 
     def dy_copy(i):
         slot = gd.at[x, y]
-        return send_to(slot, slot, dy_ss.at[i], dy_rs.at[i], on_y(i))
-
-    def dy_arrival(i):
-        slot = gd.at[x, wrap(y - i, ny)]
-        return send_to(slot, slot, dy_ss.at[i], dy_rs.at[i], on_y(i))
+        return send_to(slot, slot, dy_ss, dy_rs, on_y(i))
+
+    def dy_all():
+        slots = gd.at[x, pl.ds(0, ny - 1)]
+        return send_to(slots, slots, dy_ss, dy_rs, on_y(1))
 
     def after_h():
-        @pl.loop(1, nt)
-        def _(i):
-            h_arrival(i).wait_recv()
+        h_all().wait_recv()
 
         for c in range(s_per):
             tile = h_l[c]
@@ -595,15 +592,13 @@
             dy_copy(i).start()
 
     def after_dy():
-        @pl.loop(1, ny)
-        def _(i):
-            dy_arrival(i).wait_recv()
+        dy_all().wait_recv()
 
         start_x(dx_copy)
 
-    products(0, min(3, nz))
+    products(0, 1)
     send_rk()
-    after_ex()
+    products(1, min(3, nz))
     ring_start()
     plan = []
     if half > 1:
@@ -614,15 +609,16 @@
             plan.append((5.9 + 5.2 * (step - 2) + 1.3 * n, functools.partial(ring_step, step, n)))
     plan += [
         (0.3, lambda: products(min(3, nz), nz)),
-        (2.2, after_rk),
-        (3.0, after_f),
-        (4.0, after_r),
-        (6.0, after_h),
-        (8.4, after_u),
-        (10.6, after_dy),
-        (13.0, lambda: pass_x(ux_copy, ux_arrival, 0)),
-        (15.2, lambda: pass_x(dx_copy, dx_arrival, 0)),
-        (16.5, lambda: pass_x(ux_copy, ux_arrival, 1)),
+        (1.5, after_ex),
+        (2.5, after_rk),
+        (4.0, after_f),
+        (5.0, after_r),
+        (7.5, after_h),
+        (9.5, after_u),
+        (12.0, after_dy),
+        (13.5, lambda: pass_x(ux_copy, ux_arrival, 0)),
+        (16.0, lambda: pass_x(dx_copy, dx_arrival, 0)),
+        (17.0, lambda: pass_x(ux_copy, ux_arrival, 1)),
     ]
     plan.sort(key=lambda item: item[0])
     for _, action in plan:
@@ -633,10 +629,10 @@
     norm, scaling = norms["norm"], norms["scaling"]
 
     def pr_copy(p, j):
-        return send_to(proj_s.at[p, j], proj_l.at[y_par, j], pr_ss.at[p, j], pr_rs.at[y_par, j], on_swap(p))
-
-    def pr_arrival(p, j):
-        return send_to(proj_l.at[p, j], proj_l.at[p, j], pr_ss.at[p, j], pr_rs.at[p, j], on_swap(p))
+        return send_to(proj_s.at[p, j], proj_l.at[y_par, j], pr_ss.at[p], pr_rs.at[y_par], on_swap(p))
+
+    def pr_all(p):
+        return send_to(proj_l.at[p], proj_l.at[p], pr_ss.at[p], pr_rs.at[p], on_swap(p))
 
     sib_arrival(nz - 1).wait_recv()
     mag_sum = [None, None]
@@ -669,14 +665,14 @@
     for j in (0, 1):
         m_s[j:j + 1, :] = mag_sum[j] / norm[:, j * hb:(j + 1) * hb]
 
+    own_m = (x * s_per + cl) * 2 + y_par
+
     def m_copy(i):
-        return send_to(m_s, m_g.at[x, cl, y_par], m_ss.at[i], m_rs.at[x, cl, y_par], target(i))
-
-    def m_arrival(i):
-        xb, rest = lax.div(i, ny), lax.rem(i, ny)
-        c, p = lax.div(rest, 2), lax.rem(rest, 2)
-        slot = m_g.at[xb, c, p]
-        return send_to(slot, slot, m_ss.at[i], m_rs.at[xb, c, p], target(i))
+        return send_to(m_s, m_g.at[own_m], m_ss, m_rs, target(i))
+
+    def m_all(count):
+        slots = m_g.at[pl.ds(0, count)]
+        return send_to(slots, slots, m_ss, m_rs, on_x(1))
 
     def not_self(i):
         return jnp.logical_not(jnp.logical_and(at_home, i == dp))
@@ -689,56 +685,33 @@
 
     @pl.when(at_home)
     def _():
-        m_g[x, cl, y_par] = m_s[...]
-
-    pass_x(dx_copy, dx_arrival, 1)
-    gd_write = pltpu.make_async_copy(gd, gd_out, out_s.at[1])
-    gd_write.start()
+        m_g[own_m] = m_s[...]
 
     def proj_write(p, j):
         return pltpu.make_async_copy(
             proj_l.at[p, j], proj_out.at[:, pl.ds(p * cb + j * hb, hb)], out_s.at[2 + 2 * p + j]
         )
 
-    for flow in (0, 1):
-        for step in range(ny // 2):
-            for h in halves(flow, step, ny, pieces):
-                tok_copy(flow, step, h).wait_send()
-        for step in range(nx // 2):
-            for h in halves(flow, step, nx, pieces):
-                w_copy(flow, step, h).wait_send()
-            for h in halves(flow, step, nx, 2):
-                ux_copy(flow, step, h).wait_send()
-                dx_copy(flow, step, h).wait_send()
-        for step in range(half):
-            for q in range(4):
-                if ring_has(flow, step, q):
-                    ring_copy(flow, step, q).wait_send()
-
-    @pl.loop(1, nt)
-    def _(i):
-        ex_copy(i).wait_send()
-        rk_copy(i).wait_send()
-        h_copy(i).wait_send()
-
-    @pl.loop(0, nz)
-    def _(i):
-        sib_copy(i).wait_send()
-
-    @pl.loop(1, ny)
-    def _(i):
-        f_copy(i).wait_send()
-        r_copy(i).wait_send()
-        dy_copy(i).wait_send()
-
-    @pl.loop(0, ny)
-    def _(y2):
-        @pl.when(jnp.logical_not(jnp.logical_and(at_home, y2 == y)))
-        def _():
-            u_copy(y2).wait_send()
-
-    for i in range(1, nx):
-        up_copy(i).wait_send()
+    pass_x(dx_copy, dx_arrival, 1)
+    gd_write = pltpu.make_async_copy(gd, gd_out, out_s.at[1])
+    gd_write.start()
+
+    def left(ref, send_sem, recv_sem):
+        send_to(ref, ref, send_sem, recv_sem, on_y(1)).wait_send()
+
+    left(tok_g.at[pl.ds(0, ny - 1)], tok_ss, tok_rs.at[0])
+    left(w_g.at[pl.ds(0, nx - 1)], w_ss, w_rs.at[0])
+    left(gu.at[pl.ds(0, nx - 1)], ux_ss, ux_rs.at[0])
+    left(parts.at[pl.ds(0, nz - 1)], ring_ss, ring_rs.at[0])
+    left(parts.at[pl.ds(0, nz)], sib_ss, sib_rs.at[0])
+    up_all().wait_send()
+    ex_all().wait_send()
+    rk_all().wait_send()
+    f_all().wait_send()
+    r_all().wait_send()
+    h_all().wait_send()
+    dy_all().wait_send()
+    by_home(lambda count: u_all(count).wait_send(), ny)
     for p in (0, 1):
         @pl.when(jnp.logical_not(stays[p]))
         def _():
@@ -746,21 +719,17 @@
             mag_copy(p).wait_send()
 
     for p in (0, 1):
+        @pl.when(jnp.logical_not(stays[p]))
+        def _():
+            pr_all(p).wait_recv()
+            pr_all(p).wait_send()
+
         for j in (0, 1):
-            @pl.when(jnp.logical_not(stays[p]))
-            def _():
-                pr_arrival(p, j).wait_recv()
-                pr_copy(p, j).wait_send()
-
             proj_write(p, j).start()
 
-    @pl.loop(0, outs)
-    def _(i):
-        @pl.when(not_self(i))
-        def _():
-            m_arrival(i).wait_recv()
-            m_copy(i).wait_send()
-
+    by_home(lambda count: m_all(count).wait_recv(), outs)
+    by_home(lambda count: m_all(count).wait_send(), outs)
+    left(gd.at[pl.ds(0, nx - 1)], dx_ss, dx_rs.at[0])
     m_write = pltpu.make_async_copy(m_g, m_out, out_s.at[6])
     m_write.start()
     gu_write.wait()
@@ -771,34 +740,48 @@
     m_write.wait()
 
 
-def scatter_kernel(nx, ny, tenant, proj, gu_in, gd_in, m_in, proj_out, down_out, up_out, mag_out, gu, gd, m, sems):
+def scatter_kernel(
+    nx, ny, tenant_in, proj_in, gu_in, gd_in, m_in, proj_out, down_out, up_out, mag_out,
+    tenant, proj, gu, gd, m, down, up, mag, sems,
+):
     s_per = ny // 2
     rpy = RANK // ny
-    copies = [
-        pltpu.make_async_copy(src, dst, sems.at[n])
-        for n, (src, dst) in enumerate(((gu_in, gu), (gd_in, gd), (m_in, m), (proj, proj_out)))
-    ]
-    for copy in copies:
-        copy.start()
-    down_out[...] = jnp.zeros_like(down_out)
-    up_out[...] = jnp.zeros_like(up_out)
-    for copy in copies:
-        copy.wait()
-    hb = m.shape[4]
-    row_ids = lax.broadcasted_iota(jnp.int32, (mag_out.shape[0], hb), 0)
-    mag_sums = [jnp.zeros(row_ids.shape, F32)] * 4
-    for xb in range(nx):
-        for c in range(s_per):
-            who = tenant[xb * s_per + c]
-            for p in (0, 1):
-                up_out[who, :, 2 * hb * p:2 * hb * (p + 1)] += gu[xb, c, p]
-                for j in (0, 1):
-                    row = m[xb, c, p, j:j + 1, :]
-                    mag_sums[2 * p + j] = mag_sums[2 * p + j] + jnp.where(row_ids == who, row, 0.0)
-            rows = [gd[xb, yb, c * rpy:(c + 1) * rpy, :] for yb in range(ny)]
-            down_out[who] += jnp.concatenate(rows, axis=0)
+    hb = m.shape[2]
+    cb = 2 * hb
+    ins = ((tenant_in, tenant), (gu_in, gu), (gd_in, gd), (m_in, m), (proj_in, proj))
+    outs = ((up, up_out), (down, down_out), (mag, mag_out), (proj, proj_out))
+    reads = [pltpu.make_async_copy(src, dst, sems.at[n]) for n, (src, dst) in enumerate(ins)]
+    writes = [pltpu.make_async_copy(src, dst, sems.at[5 + n]) for n, (src, dst) in enumerate(outs)]
+    for read in reads:
+        read.start()
+    up[...] = jnp.zeros_like(up)
+    down[...] = jnp.zeros_like(down)
+    reads[0].wait()
+    who = [tenant[n] for n in range(nx * s_per)]
+    reads[1].wait()
+    for n in range(nx * s_per):
+        for p in (0, 1):
+            up[who[n], :, cb * p:cb * (p + 1)] += gu[n // s_per, 2 * (n % s_per) + p]
+    writes[0].start()
+    reads[2].wait()
+    for n in range(nx * s_per):
+        c = n % s_per
+        rows = [gd[n // s_per, yb, c * rpy:(c + 1) * rpy, :] for yb in range(ny)]
+        down[who[n]] += jnp.concatenate(rows, axis=0)
+    writes[1].start()
+    reads[4].wait()
+    writes[3].start()
+    reads[3].wait()
+    row_ids = lax.broadcasted_iota(jnp.int32, (mag.shape[0], hb), 0)
+    sums = [jnp.zeros(row_ids.shape, F32)] * 4
+    for n in range(nx * s_per):
+        for q in range(4):
+            sums[q] = sums[q] + jnp.where(row_ids == who[n], m[2 * n + q // 2, q % 2:q % 2 + 1, :], 0.0)
     for q in range(4):
-        mag_out[:, hb * q:hb * (q + 1)] = mag_sums[q]
+        mag[:, hb * q:hb * (q + 1)] = sums[q]
+    writes[2].start()
+    for write in writes:
+        write.wait()
 
 
 def per_device(nx, ny, nt, tokens, base_weight, adapter_down, adapter_up, magnitude, tenant, cotangent):
@@ -811,9 +794,9 @@
     rpy = RANK // ny
     dma = pltpu.SemaphoreType.DMA
     vmem = pl.BlockSpec(memory_space=pltpu.VMEM)
-    smem = pl.BlockSpec(memory_space=pltpu.SMEM)
     hbm = pl.BlockSpec(memory_space=pltpu.HBM)
     scratch = [
+        pltpu.SMEM(tenant.shape, jnp.int32),
         pltpu.VMEM(adapter_down.shape, BF16),
         pltpu.VMEM(adapter_up.shape, BF16),
         pltpu.VMEM(magnitude.shape, F32),
@@ -843,34 +826,32 @@
         pltpu.VMEM((nt, 2 * rpy, tb), F32),
         pltpu.VMEM((RANK, 2 * tb), F32),
         pltpu.VMEM((RANK, cb), F32),
-        pltpu.VMEM((nx, s_per, 2, RANK, cb), F32),
+        pltpu.VMEM((nx, ny, RANK, cb), F32),
         pltpu.VMEM((nx, ny, s_per * rpy, kb), F32),
         pltpu.VMEM((2 * tb, cb), F32),
         pltpu.VMEM((2, 2, tb, hb), BF16),
         pltpu.VMEM((2, 2, tb, hb), BF16),
         pltpu.VMEM((2, hb), F32),
-        pltpu.VMEM((nx, s_per, 2, 2, hb), F32),
-        dma((6,)),
+        pltpu.VMEM((nx * ny, 2, hb), F32),
+        dma((7,)),
     ]
+    tok_n, w_n, x_n, ring_n = 4 * (ny - 1), 4 * (nx - 1), 2 * (nx - 1), 4 * (nz - 1)
     pairs = [
-        ((2, ny // 2, 4),) * 2, ((2, nx // 2, 4),) * 2, ((nx,),) * 2, ((2,),) * 2, ((2,),) * 2,
-        ((nt,),) * 2, ((nt,),) * 2, ((nz,),) * 2, ((2, nz // 2, 4),) * 2,
-        ((ny,),) * 2, ((ny,),) * 2, ((nt,),) * 2,
-        ((ny,), (s_per, 2)), ((2, nx // 2, 2),) * 2, ((ny,),) * 2, ((2, nx // 2, 2),) * 2,
-        ((2, 2),) * 2, ((nx * ny,), (nx, s_per, 2)),
+        (1, tok_n), (1, w_n), (1, 1), (2, 2), (2, 2), (1, 1), (1, 1), (1, nz), (1, ring_n),
+        (1, 1), (1, 1), (1, 1), (1, 1), (1, x_n), (1, 1), (1, x_n), (2, 2), (1, 1),
     ]
-    for first, second in pairs:
-        scratch += [dma(first), dma(second)]
+    for pair in pairs:
+        scratch += [dma if count == 1 else dma((count,)) for count in pair]
     scratch.append(dma((7,)))
     proj, up_terms, down_terms, mags = pl.pallas_call(
         functools.partial(exchange_kernel, nx, ny, nt),
         out_shape=(
             jax.ShapeDtypeStruct((tb, 2 * cb), BF16),
-            jax.ShapeDtypeStruct((nx, s_per, 2, RANK, cb), F32),
+            jax.ShapeDtypeStruct((nx, ny, RANK, cb), F32),
             jax.ShapeDtypeStruct((nx, ny, s_per * rpy, kb), F32),
-            jax.ShapeDtypeStruct((nx, s_per, 2, 2, hb), F32),
+            jax.ShapeDtypeStruct((nx * ny, 2, hb), F32),
         ),
-        in_specs=[smem] + [hbm] * 6,
+        in_specs=[hbm] * 7,
         out_specs=(hbm,) * 4,
         scratch_shapes=scratch,
         compiler_params=pltpu.CompilerParams(
@@ -886,13 +867,18 @@
             jax.ShapeDtypeStruct((tenants, RANK, 2 * cb), F32),
             jax.ShapeDtypeStruct((tenants, 2 * cb), F32),
         ),
-        in_specs=[smem] + [hbm] * 4,
-        out_specs=(hbm, vmem, vmem, vmem),
+        in_specs=[hbm] * 5,
+        out_specs=(hbm,) * 4,
         scratch_shapes=[
+            pltpu.SMEM(tenant.shape, jnp.int32),
+            pltpu.VMEM(proj.shape, BF16),
             pltpu.VMEM(up_terms.shape, F32),
             pltpu.VMEM(down_terms.shape, F32),
             pltpu.VMEM(mags.shape, F32),
-            dma((4,)),
+            pltpu.VMEM((tenants, RANK, kb), F32),
+            pltpu.VMEM((tenants, RANK, 2 * cb), F32),
+            pltpu.VMEM((tenants, 2 * cb), F32),
+            dma((9,)),
         ],
         compiler_params=pltpu.CompilerParams(vmem_limit_bytes=60 * 1024 * 1024),
         name="scatter",

time: 84.7 us -> 74.9 us (0.88)
  Pallas kernels: 83.9 us -> 73.8 us
    pallas_call x1, Pallas kernels: 76.6 us -> 71.2 us  [per_device(): pl.pallas_call(functools.partial(exchange_kernel, nx, ny, nt), out_shape=...]
    pallas_call x1, Pallas kernels: 7.23 us -> 2.56 us  [per_device(): pl.pallas_call(functools.partial(scatter_kernel, nx, ny), out_shape=(jax....]
where the time goes in v3:
time: 74.9 us; the launch traced here: 74.4 us
  Pallas kernels  73.8 us (99%)
    pallas_call x1, Pallas kernels, per_device(): pl.pallas_call(functools.partial(exchange_kernel, nx, ny, nt), out_shape=...  71.2 us
    pallas_call x1, Pallas kernels, per_device(): pl.pallas_call(functools.partial(scatter_kernel, nx, ny), out_shape=(jax....  2.56 us

profile of v3, /device:TPU:1, one launch (start us, length us, event | category | flops | bytes accessed | tf_op | source)
XLA Modules:
  0.0 74.4 jit_solution(17618436713579608863)
XLA Ops:
  0.6 71.2 %exchange.1 = (bf16[128,512]{1,0:T(8,128)(2,1)}, f32[4,8,16,256]{3,2,1,0:T(8,128)}, f32[4,8,8,512]{3,2,1,0:T(8,128)}, f32[32,2,128]{2,1,0:T(2,128)}) custom-call(s32[16]{0:T(128)} %tenant_in.3, bf16[128,512]{1,0:T(8,128)(2,1)} %tok.1, bf16[512,256]{1,0:T(8,128)(2,1)} %w.1, bf16[32,16,512]{2,1,0:T(8,128)(2,1)} %down.1, bf16[32,16,256]{2,1,0:T(8,128)(2,1)} %up.1, ...), custom_call_target="tpu_custom_call" | custom-call | tf_op jit(solution)/shard_map/exchange/pallas_call | solution.py:846
  71.9 2.6 %scatter.1 = (bf16[128,512]{1,0:T(8,128)(2,1)}, f32[32,16,512]{2,1,0:T(8,128)}, f32[32,16,512]{2,1,0:T(8,128)}, f32[32,512]{1,0:T(8,128)}) custom-call(s32[16]{0:T(128)} %tenant_in.3, bf16[128,512]{1,0:T(8,128)(2,1)} %get-tuple-element.8.proj_in, f32[4,8,16,256]{3,2,1,0:T(8,128)} %get-tuple-element.9.gu_in, f32[4,8,8,512]{3,2,1,0:T(8,128)} %get-tuple-element.10.gd_in, ...), custom_call_target="tpu_custom_call" | custom-call | tf_op jit(solution)/shard_map/scatter/pallas_call | solution.py:862

commit v4 on v3

--- a/solution.py
+++ b/solution.py
@@ -65,7 +65,7 @@
     ex_s, ex_l, rk_s, rk_l, rank_p, parts, sib, ring,
     scaled_s, f_s, f_l, r_s, r_l, h_s, h_l, rank_s, u_s, gu, gd, low_s, proj_s, proj_l, m_s, m_g,
     in_s, tok_ss, tok_rs, w_ss, w_rs, up_ss, up_rs, cot_ss, cot_rs, mag_ss, mag_rs,
-    ex_ss, ex_rs, rk_ss, rk_rs, sib_ss, sib_rs, ring_ss, ring_rs, f_ss, f_rs, r_ss, r_rs, h_ss, h_rs,
+    ex_ss, ex_rs, rk_ss, rk_rs, sib_ss, sib_rs, first_rs, ring_ss, ring_rs, f_ss, f_rs, r_ss, r_rs, h_ss, h_rs,
     u_ss, u_rs, ux_ss, ux_rs, dy_ss, dy_rs, dx_ss, dx_rs, pr_ss, pr_rs, m_ss, m_rs, out_s,
 ):
     s_per = ny // 2
@@ -138,7 +138,7 @@
     outs = nx * ny
 
     def target(i):
-        return (i, t_out)
+        return (wrap(dp + i, outs), t_out)
 
     for xb in range(nx):
         for c in range(s_per):
@@ -148,6 +148,60 @@
                 @pl.when(jnp.logical_not(jnp.logical_and(maker[0] == dp, maker[1] == t)))
                 def _():
                     greet(maker)
+
+    others = (ny - 1) + (nx - 1) + (nt - 1)
+
+    @pl.when(at_home)
+    def _():
+        pl.semaphore_wait(barrier, others + outs - 1)
+
+    @pl.when(away)
+    def _():
+        pl.semaphore_wait(barrier, others + outs)
+
+    pieces = 4
+    tp, wp = tb // pieces, kb // pieces
+
+    def sign_of(flow):
+        return 1 if flow == 0 else -1
+
+    def at(count, many, flow, step, h):
+        before = sum(len(halves(flow, k, count, many)) for k in range(step))
+        place = halves(flow, step, count, many).index(h)
+        return flow * (count - 1) * many // 2 + before + place
+
+    def tok_copy(flow, step, h):
+        sign = sign_of(flow)
+        slot = tok_g.at[wrap(y - sign * step, ny), pl.ds(h * tp, tp)]
+        src = tok.at[pl.ds(h * tp, tp)] if step == 0 else slot
+        return send_to(src, slot, tok_ss, tok_rs.at[at(ny, pieces, flow, step, h)], on_y(sign))
+
+    def tok_arrival(flow, step, h):
+        sign = sign_of(flow)
+        slot = tok_g.at[wrap(y - sign * (step + 1), ny), pl.ds(h * tp, tp)]
+        return send_to(slot, slot, tok_ss, tok_rs.at[at(ny, pieces, flow, step, h)], on_y(sign))
+
+    def w_copy(flow, step, h):
+        sign = sign_of(flow)
+        slot = w_g.at[wrap(x - sign * step, nx), pl.ds(h * wp, wp)]
+        src = w.at[pl.ds(h * wp, wp)] if step == 0 else slot
+        return send_to(src, slot, w_ss, w_rs.at[at(nx, pieces, flow, step, h)], on_x(sign))
+
+    def w_arrival(flow, step, h):
+        sign = sign_of(flow)
+        slot = w_g.at[wrap(x - sign * (step + 1), nx), pl.ds(h * wp, wp)]
+        return send_to(slot, slot, w_ss, w_rs.at[at(nx, pieces, flow, step, h)], on_x(sign))
+
+    def up_copy(i):
+        return send_to(up_sel.at[wrap(x + i, nx)], up_g.at[x], up_ss, up_rs, on_x(i))
+
+    def up_all():
+        slots = up_g.at[pl.ds(0, nx - 1)]
+        return send_to(slots, slots, up_ss, up_rs, on_x(1))
+
+    for flow in (0, 1):
+        tok_copy(flow, 0, send_order(flow, 0, ny, pieces)[0]).start()
+        w_copy(flow, 0, send_order(flow, 0, nx, pieces)[0]).start()
 
     for n in (6, 1, 2, 3):
         fetches[n].wait()
@@ -161,57 +215,10 @@
     for p in (0, 1):
         mag_s[p] = jnp.broadcast_to(mag_row[:, p * cb:(p + 1) * cb], (8, cb))
 
-    others = (ny - 1) + (nx - 1) + (nt - 1)
-
-    @pl.when(at_home)
-    def _():
-        pl.semaphore_wait(barrier, others + outs - 1)
-
-    @pl.when(away)
-    def _():
-        pl.semaphore_wait(barrier, others + outs)
-
-    pieces = 4
-    tp, wp = tb // pieces, kb // pieces
-
-    def sign_of(flow):
-        return 1 if flow == 0 else -1
-
-    def at(count, many, flow, step, h):
-        before = sum(len(halves(flow, k, count, many)) for k in range(step))
-        place = halves(flow, step, count, many).index(h)
-        return flow * (count - 1) * many // 2 + before + place
-
-    def tok_copy(flow, step, h):
-        sign = sign_of(flow)
-        slot = tok_g.at[wrap(y - sign * step, ny), pl.ds(h * tp, tp)]
-        src = tok.at[pl.ds(h * tp, tp)] if step == 0 else slot
-        return send_to(src, slot, tok_ss, tok_rs.at[at(ny, pieces, flow, step, h)], on_y(sign))
-
-    def tok_arrival(flow, step, h):
-        sign = sign_of(flow)
-        slot = tok_g.at[wrap(y - sign * (step + 1), ny), pl.ds(h * tp, tp)]
-        return send_to(slot, slot, tok_ss, tok_rs.at[at(ny, pieces, flow, step, h)], on_y(sign))
-
-    def w_copy(flow, step, h):
-        sign = sign_of(flow)
-        slot = w_g.at[wrap(x - sign * step, nx), pl.ds(h * wp, wp)]
-        src = w.at[pl.ds(h * wp, wp)] if step == 0 else slot
-        return send_to(src, slot, w_ss, w_rs.at[at(nx, pieces, flow, step, h)], on_x(sign))
-
-    def w_arrival(flow, step, h):
-        sign = sign_of(flow)
-        slot = w_g.at[wrap(x - sign * (step + 1), nx), pl.ds(h * wp, wp)]
-        return send_to(slot, slot, w_ss, w_rs.at[at(nx, pieces, flow, step, h)], on_x(sign))
-
-    def up_copy(i):
-        return send_to(up_sel.at[wrap(x + i, nx)], up_g.at[x], up_ss, up_rs, on_x(i))
-
-    def up_all():
-        slots = up_g.at[pl.ds(0, nx - 1)]
-        return send_to(slots, slots, up_ss, up_rs, on_x(1))
-
-    for place in range(pieces):
+    for i in range(1, nx):
+        up_copy(i).start()
+
+    for place in range(1, pieces):
         for flow in (0, 1):
             order = send_order(flow, 0, ny, pieces)
             if place < len(order):
@@ -219,9 +226,6 @@
             order = send_order(flow, 0, nx, pieces)
             if place < len(order):
                 w_copy(flow, 0, order[place]).start()
-        if place == 0:
-            for i in range(1, nx):
-                up_copy(i).start()
 
     def cot_copy(p):
         return send_to(cot_v.at[:, pl.ds(p * cb, cb)], cot_l.at[y_par], cot_ss.at[p], cot_rs.at[y_par], on_swap(p))
@@ -364,6 +368,10 @@
         slot = sib.at[place_of(i)]
         return send_to(slot, slot, sib_ss, sib_rs.at[i], sibling)
 
+    def first_copy(q):
+        zb = place_of(0)
+        return send_to(parts.at[2 * zb + 1 - core, q], sib.at[zb, q], sib_ss, first_rs.at[q], sibling)
+
     def products(first, end):
         @pl.loop(first, end)
         def _(i):
@@ -396,18 +404,23 @@
 
     ring_order = ((2, 3, 0, 1), (0, 1, 2, 3))
 
+    def order_at(flow, step):
+        return ring_order[flow] if step < 2 else (0, 1, 2, 3)
+
+
     def ring_start():
-        sib_arrival(0).wait_recv()
         for n in (2, 3):
             for flow in (0, 1):
-                ring_send(flow, 0, ring_order[flow][n])
+                q = ring_order[flow][n]
+                first_copy(q).wait_recv()
+                ring_send(flow, 0, q)
 
     def ring_step(step, n):
         if n == 0:
             sib_arrival(2 * step - 1).wait_recv()
             sib_arrival(2 * step).wait_recv()
         for flow in (0, 1):
-            ring_send(flow, step, ring_order[flow][n])
+            ring_send(flow, step, order_at(flow, step)[n])
 
     norms = {}
 
@@ -596,7 +609,11 @@
 
         start_x(dx_copy)
 
-    products(0, 1)
+    product(2 * place_of(0) + 1 - core)
+    for n in (2, 3):
+        for flow in (0, 1):
+            first_copy(ring_order[flow][n]).start()
+    product(2 * place_of(0) + core)
     send_rk()
     products(1, min(3, nz))
     ring_start()
@@ -608,7 +625,8 @@
         for n in range(4):
             plan.append((5.9 + 5.2 * (step - 2) + 1.3 * n, functools.partial(ring_step, step, n)))
     plan += [
-        (0.3, lambda: products(min(3, nz), nz)),
+        (0.3, lambda: products(min(3, nz), min(5, nz))),
+        (4.7, lambda: products(min(5, nz), nz)),
         (1.5, after_ex),
         (2.5, after_rk),
         (4.0, after_f),
@@ -634,31 +652,36 @@
     def pr_all(p):
         return send_to(proj_l.at[p], proj_l.at[p], pr_ss.at[p], pr_rs.at[p], on_swap(p))
 
+    def send_pr(p, j):
+        @pl.when(jnp.logical_not(stays[p]))
+        def _():
+            pr_copy(p, j).start()
+
+        @pl.when(stays[p])
+        def _():
+            proj_l[p, j] = proj_s[p, j]
+
     sib_arrival(nz - 1).wait_recv()
+    for q in range(4):
+        p, j = q // 2, q % 2
+        parts[t, q] = parts[t, q] + sib[z, q] + low_s[p * tb:(p + 1) * tb, j * hb:(j + 1) * hb]
     mag_sum = [None, None]
     for n in range(4):
         for flow in (0, 1):
-            q = ring_order[flow][n]
+            q = order_at(flow, half - 1)[n]
             if ring_has(flow, half - 1, q):
                 ring_copy(flow, half - 1, q).wait_recv()
-        for q in ([0, 2] if n == 2 else [1, 3] if n == 3 else []):
+        for q in ([n] if half > 2 else [0, 2] if n == 2 else [1, 3] if n == 3 else []):
             p, j = q // 2, q % 2
             lanes = slice(j * hb, (j + 1) * hb)
-            value = parts[t, q] + sib[z, q]
+            value = parts[t, q]
             for flow in (0, 1):
                 if ring_has(flow, half - 1, q):
                     value = value + ring[flow, half - 1, q]
-            value = value + low_s[p * tb:(p + 1) * tb, lanes]
             proj_s[p, j] = (value * scaling[:, lanes]).astype(BF16)
 
-            @pl.when(jnp.logical_not(stays[p]))
-            def _():
-                pr_copy(p, j).start()
-
-            @pl.when(stays[p])
-            def _():
-                proj_l[p, j] = proj_s[p, j]
-
+            if n < 3:
+                send_pr(p, j)
             term = jnp.sum(cot_l[p, :, lanes].astype(F32) * value, axis=0, keepdims=True)
             mag_sum[j] = term if mag_sum[j] is None else mag_sum[j] + term
 
@@ -674,23 +697,34 @@
         slots = m_g.at[pl.ds(0, count)]
         return send_to(slots, slots, m_ss, m_rs, on_x(1))
 
-    def not_self(i):
-        return jnp.logical_not(jnp.logical_and(at_home, i == dp))
-
-    @pl.loop(0, outs)
-    def _(i):
-        @pl.when(not_self(i))
-        def _():
-            m_copy(i).start()
+    for i in range(1, outs):
+        m_copy(i).start()
+
+    @pl.when(away)
+    def _():
+        m_copy(0).start()
 
     @pl.when(at_home)
     def _():
         m_g[own_m] = m_s[...]
+
+    for q in (3,) if half > 2 else (1, 3):
+        send_pr(q // 2, q % 2)
 
     def proj_write(p, j):
         return pltpu.make_async_copy(
             proj_l.at[p, j], proj_out.at[:, pl.ds(p * cb + j * hb, hb)], out_s.at[2 + 2 * p + j]
         )
+
+    for p in (0, 1):
+        @pl.when(jnp.logical_not(stays[p]))
+        def _():
+            pr_all(p).wait_recv()
+            pr_all(p).wait_send()
+
+        for j in (0, 1):
+            proj_write(p, j).start()
+
 
     pass_x(dx_copy, dx_arrival, 1)
     gd_write = pltpu.make_async_copy(gd, gd_out, out_s.at[1])
@@ -717,15 +751,6 @@
         def _():
             cot_copy(p).wait_send()
             mag_copy(p).wait_send()
-
-    for p in (0, 1):
-        @pl.when(jnp.logical_not(stays[p]))
-        def _():
-            pr_all(p).wait_recv()
-            pr_all(p).wait_send()
-
-        for j in (0, 1):
-            proj_write(p, j).start()
 
     by_home(lambda count: m_all(count).wait_recv(), outs)
     by_home(lambda count: m_all(count).wait_send(), outs)
@@ -840,8 +865,10 @@
         (1, tok_n), (1, w_n), (1, 1), (2, 2), (2, 2), (1, 1), (1, 1), (1, nz), (1, ring_n),
         (1, 1), (1, 1), (1, 1), (1, 1), (1, x_n), (1, 1), (1, x_n), (2, 2), (1, 1),
     ]
-    for pair in pairs:
+    for place, pair in enumerate(pairs):
         scratch += [dma if count == 1 else dma((count,)) for count in pair]
+        if place == 7:
+            scratch.append(dma((4,)))
     scratch.append(dma((7,)))
     proj, up_terms, down_terms, mags = pl.pallas_call(
         functools.partial(exchange_kernel, nx, ny, nt),

time: 74.9 us -> 73.3 us (0.979)
  Pallas kernels: 73.8 us -> 72.2 us
    pallas_call x1, Pallas kernels: 71.2 us -> 69.7 us  [per_device(): pl.pallas_call(functools.partial(exchange_kernel, nx, ny, nt), out_shape=...]
where the time goes in v4:
time: 73.3 us; the launch traced here: 72.9 us
  Pallas kernels  72.2 us (98%)
    pallas_call x1, Pallas kernels, per_device(): pl.pallas_call(functools.partial(exchange_kernel, nx, ny, nt), out_shape=...  69.7 us
    pallas_call x1, Pallas kernels, per_device(): pl.pallas_call(functools.partial(scatter_kernel, nx, ny), out_shape=(jax....  2.57 us

profile of v4, /device:TPU:1, one launch (start us, length us, event | category | flops | bytes accessed | tf_op | source)
XLA Modules:
  0.0 72.9 jit_solution(3460848957912409698)
XLA Ops:
  0.6 69.7 %exchange.1 = (bf16[128,512]{1,0:T(8,128)(2,1)}, f32[4,8,16,256]{3,2,1,0:T(8,128)}, f32[4,8,8,512]{3,2,1,0:T(8,128)}, f32[32,2,128]{2,1,0:T(2,128)}) custom-call(s32[16]{0:T(128)} %tenant_in.3, bf16[128,512]{1,0:T(8,128)(2,1)} %tok.1, bf16[512,256]{1,0:T(8,128)(2,1)} %w.1, bf16[32,16,512]{2,1,0:T(8,128)(2,1)} %down.1, bf16[32,16,256]{2,1,0:T(8,128)(2,1)} %up.1, ...), custom_call_target="tpu_custom_call" | custom-call | tf_op jit(solution)/shard_map/exchange/pallas_call | solution.py:873
  70.3 2.6 %scatter.1 = (bf16[128,512]{1,0:T(8,128)(2,1)}, f32[32,16,512]{2,1,0:T(8,128)}, f32[32,16,512]{2,1,0:T(8,128)}, f32[32,512]{1,0:T(8,128)}) custom-call(s32[16]{0:T(128)} %tenant_in.3, bf16[128,512]{1,0:T(8,128)(2,1)} %get-tuple-element.8.proj_in, f32[4,8,16,256]{3,2,1,0:T(8,128)} %get-tuple-element.9.gu_in, f32[4,8,8,512]{3,2,1,0:T(8,128)} %get-tuple-element.10.gd_in, ...), custom_call_target="tpu_custom_call" | custom-call | tf_op jit(solution)/shard_map/scatter/pallas_call | solution.py:889

commit v5 on v4

--- a/solution.py
+++ b/solution.py
@@ -63,9 +63,9 @@
     proj_out, gu_out, gd_out, m_out,
     tenant, down_v, up_v, mag_v, cot_v, tok_g, w_g, up_sel, up_g, down_sel, cot_l, mag_s, mag_l,
     ex_s, ex_l, rk_s, rk_l, rank_p, parts, sib, ring,
-    scaled_s, f_s, f_l, r_s, r_l, h_s, h_l, rank_s, u_s, gu, gd, low_s, proj_s, proj_l, m_s, m_g,
+    scaled_s, f_s, f_l, h_s, h_l, rank_s, u_s, gu, gd, low_s, proj_s, proj_l, m_s, m_g,
     in_s, tok_ss, tok_rs, w_ss, w_rs, up_ss, up_rs, cot_ss, cot_rs, mag_ss, mag_rs,
-    ex_ss, ex_rs, rk_ss, rk_rs, sib_ss, sib_rs, first_rs, ring_ss, ring_rs, f_ss, f_rs, r_ss, r_rs, h_ss, h_rs,
+    ex_ss, ex_rs, rk_ss, rk_rs, sib_ss, sib_rs, first_rs, ring_ss, ring_rs, f_ss, f_rs, h_ss, h_rs,
     u_ss, u_rs, ux_ss, ux_rs, dy_ss, dy_rs, dx_ss, dx_rs, pr_ss, pr_rs, m_ss, m_rs, out_s,
 ):
     s_per = ny // 2
@@ -442,7 +442,10 @@
         rows = up_g[xq, cl]
         parts3 = split3(scaled)
         back = dot_nt(rows, parts3[0]) + (dot_nt(rows, parts3[1]) + dot_nt(rows, parts3[2]))
+        rk_all().wait_recv()
+        ranks = jnp.sum(rk_l[...], axis=0)
         for y2 in range(ny):
+            f_s[y2, 2 * rpy:4 * rpy, :] = ranks
             f_s[y2, 0:rpy, :] = back[y2 * rpy:(y2 + 1) * rpy, :tb]
             f_s[y2, rpy:2 * rpy, :] = back[y2 * rpy:(y2 + 1) * rpy, tb:]
 
@@ -460,13 +463,6 @@
         slots = f_l.at[pl.ds(0, ny - 1)]
         return send_to(slots, slots, f_ss, f_rs, on_y(1))
 
-    def r_copy(i):
-        return send_to(r_s, r_l.at[y], r_ss, r_rs, on_y(i))
-
-    def r_all():
-        slots = r_l.at[pl.ds(0, ny - 1)]
-        return send_to(slots, slots, r_ss, r_rs, on_y(1))
-
     def h_copy(i):
         return send_to(h_s, h_l.at[t], h_ss, h_rs, on_t(i))
 
@@ -474,21 +470,10 @@
         slots = h_l.at[pl.ds(0, nt - 1)]
         return send_to(slots, slots, h_ss, h_rs, on_t(1))
 
-    def after_rk():
-        rk_all().wait_recv()
-
-        r_s[...] = jnp.sum(rk_l[...], axis=0)
-
-        @pl.loop(1, ny)
-        def _(i):
-            r_copy(i).start()
-
-        r_l[y] = r_s[...]
-
     def after_f():
         f_all().wait_recv()
 
-        h_s[...] = jnp.sum(f_l[...], axis=0)
+        h_s[...] = jnp.sum(f_l[:, 0:2 * rpy, :], axis=0)
 
         @pl.loop(1, nt)
         def _(i):
@@ -513,11 +498,10 @@
             wait(count)
 
     def after_r():
-        r_all().wait_recv()
 
         for y2 in range(ny):
-            rank_s[y2 * rpy:(y2 + 1) * rpy, :tb] = r_l[y2, 0:rpy, :]
-            rank_s[y2 * rpy:(y2 + 1) * rpy, tb:] = r_l[y2, rpy:2 * rpy, :]
+            rank_s[y2 * rpy:(y2 + 1) * rpy, :tb] = f_l[y2, 2 * rpy:3 * rpy, :]
+            rank_s[y2 * rpy:(y2 + 1) * rpy, tb:] = f_l[y2, 3 * rpy:4 * rpy, :]
         a1, a2, a3 = split3(rank_s[...])
         b1, b2, b3 = split3(scaled_s[...])
         low = dot_nn(a3, b1) + dot_nn(a2, b2) + dot_nn(a1, b3)
@@ -628,7 +612,6 @@
         (0.3, lambda: products(min(3, nz), min(5, nz))),
         (4.7, lambda: products(min(5, nz), nz)),
         (1.5, after_ex),
-        (2.5, after_rk),
         (4.0, after_f),
         (5.0, after_r),
         (7.5, after_h),
@@ -742,7 +725,6 @@
     ex_all().wait_send()
     rk_all().wait_send()
     f_all().wait_send()
-    r_all().wait_send()
     h_all().wait_send()
     dy_all().wait_send()
     by_home(lambda count: u_all(count).wait_send(), ny)
@@ -843,10 +825,8 @@
         pltpu.VMEM((nz, 4, tb, hb), F32),
         pltpu.VMEM((2, nz // 2, 4, tb, hb), F32),
         pltpu.VMEM((2 * tb, cb), F32),
-        pltpu.VMEM((ny, 2 * rpy, tb), F32),
-        pltpu.VMEM((ny, 2 * rpy, tb), F32),
-        pltpu.VMEM((2 * rpy, tb), F32),
-        pltpu.VMEM((ny, 2 * rpy, tb), F32),
+        pltpu.VMEM((ny, 4 * rpy, tb), F32),
+        pltpu.VMEM((ny, 4 * rpy, tb), F32),
         pltpu.VMEM((2 * rpy, tb), F32),
         pltpu.VMEM((nt, 2 * rpy, tb), F32),
         pltpu.VMEM((RANK, 2 * tb), F32),
@@ -863,7 +843,7 @@
     tok_n, w_n, x_n, ring_n = 4 * (ny - 1), 4 * (nx - 1), 2 * (nx - 1), 4 * (nz - 1)
     pairs = [
         (1, tok_n), (1, w_n), (1, 1), (2, 2), (2, 2), (1, 1), (1, 1), (1, nz), (1, ring_n),
-        (1, 1), (1, 1), (1, 1), (1, 1), (1, x_n), (1, 1), (1, x_n), (2, 2), (1, 1),
+        (1, 1), (1, 1), (1, 1), (1, x_n), (1, 1), (1, x_n), (2, 2), (1, 1),
     ]
     for place, pair in enumerate(pairs):
         scratch += [dma if count == 1 else dma((count,)) for count in pair]

time: 73.3 us -> 73.4 us (level)
  no operation moved by 1% of the time
where the time goes in v5:
time: 73.4 us; the launch traced here: 72.4 us
  Pallas kernels  71.7 us (98%)
    pallas_call x1, Pallas kernels, per_device(): pl.pallas_call(functools.partial(exchange_kernel, nx, ny, nt), out_shape=...  69.2 us
    pallas_call x1, Pallas kernels, per_device(): pl.pallas_call(functools.partial(scatter_kernel, nx, ny), out_shape=(jax....  2.56 us

profile of v5, /device:TPU:1, one launch (start us, length us, event | category | flops | bytes accessed | tf_op | source)
XLA Modules:
  0.0 72.4 jit_solution(10167217762447137734)
XLA Ops:
  0.6 69.2 %exchange.1 = (bf16[128,512]{1,0:T(8,128)(2,1)}, f32[4,8,16,256]{3,2,1,0:T(8,128)}, f32[4,8,8,512]{3,2,1,0:T(8,128)}, f32[32,2,128]{2,1,0:T(2,128)}) custom-call(s32[16]{0:T(128)} %tenant_in.3, bf16[128,512]{1,0:T(8,128)(2,1)} %tok.1, bf16[512,256]{1,0:T(8,128)(2,1)} %w.1, bf16[32,16,512]{2,1,0:T(8,128)(2,1)} %down.1, bf16[32,16,256]{2,1,0:T(8,128)(2,1)} %up.1, ...), custom_call_target="tpu_custom_call" | custom-call | tf_op jit(solution)/shard_map/exchange/pallas_call | solution.py:853
  69.8 2.6 %scatter.1 = (bf16[128,512]{1,0:T(8,128)(2,1)}, f32[32,16,512]{2,1,0:T(8,128)}, f32[32,16,512]{2,1,0:T(8,128)}, f32[32,512]{1,0:T(8,128)}) custom-call(s32[16]{0:T(128)} %tenant_in.3, bf16[128,512]{1,0:T(8,128)(2,1)} %get-tuple-element.8.proj_in, f32[4,8,16,256]{3,2,1,0:T(8,128)} %get-tuple-element.9.gu_in, f32[4,8,8,512]{3,2,1,0:T(8,128)} %get-tuple-element.10.gd_in, ...), custom_call_target="tpu_custom_call" | custom-call | tf_op jit(solution)/shard_map/scatter/pallas_call | solution.py:869
